TPU v7x, 256 devices: a whole 4x4x8 slice. The times are simulated.
256 devices in a mesh: seq: 32 (over x, z_lo, core), dp: 8 (over z_hi, y).
Axes of the slice: x: 4, y: 4, z: 8 (z_hi: 2, z_lo: 4; z = z_hi * 4 + z_lo), core: 2. Of those that a mesh axis runs over, the one named last changes fastest.
Arguments:
- hidden_in: bfloat16 [8, 32, 256, 1152], P('dp', 'seq'), may hold values from -6 to 6
- qkv_spatial: bfloat16 [8, 32, 256, 3456], P('dp', 'seq'), may hold values from -75 to 75
- qkv_temporal: bfloat16 [8, 32, 256, 3456], P('dp', 'seq'), may hold values from -75 to 75
- grad_out: bfloat16 [8, 32, 256, 1152], P('dp', 'seq'), may hold values from -6 to 6
- grad_temporal: bfloat16 [8, 32, 256, 1152], P('dp', 'seq'), may hold values from -6 to 6
- gate_spatial: bfloat16 [8, 1152], P('dp'), may hold values from 0.5 to 2
- modulation: bfloat16 [8, 2, 1152], P('dp'), may hold values from -2.5 to 2.5
- w_out_spatial: bfloat16 [1152, 1152], P('dp'), may hold values from -0.1875 to 0.1875
- w_qkv_temporal: bfloat16 [1152, 3456], P('dp'), may hold values from -0.1875 to 0.1875
Outputs:
- grad_hidden: bfloat16 [8, 32, 256, 1152], P('dp', 'seq')
- grad_qkv_spatial: bfloat16 [8, 32, 256, 3456], P('dp', 'seq')
- grad_w_out: float32 [1152, 1152], P('dp', 'seq')
- grad_w_qkv: float32 [1152, 3456], P('dp', 'seq')
All inputs are finite; a program needn't handle non-finite values.
Results may differ from a plain program's by a relative error of at most 0.03.
Values may be sent and summed in bfloat16 or wider, within the bound.
A program may use at most 128 MiB of HBM per device.

v0:
```python
import functools
import math

import jax
import jax.numpy as jnp
from jax import lax
from jax.experimental import pallas as pl
from jax.experimental.pallas import tpu as pltpu
from jax.sharding import PartitionSpec as P

HEADS = 16
D = 1152
SEQ = 32
DP = 8
EPSILON = 1e-06
VMEM_LIMIT = 56 * 1024 * 1024
BF = jnp.bfloat16
F32 = jnp.float32


SCALE = 1.0 / math.sqrt(D // HEADS)
LOG2E = math.log2(math.e)


def nt(a, b):
    return lax.dot_general(a, b, (((1,), (1,)), ((), ())), preferred_element_type=F32)


def tn(a, b):
    return lax.dot_general(a, b, (((0,), (0,)), ((), ())), preferred_element_type=F32)


def nn(a, b):
    return jnp.dot(a, b, preferred_element_type=F32)


def window(h):
    chunk = jnp.minimum(h * 9 // 16, 7)
    lane = lax.broadcasted_iota(jnp.int32, (1, 256), 1) + chunk * 128 - h * 72
    keep = jnp.where(jnp.logical_and(lane >= 0, lane < 72), 1.0, 0.0).astype(BF)
    return chunk * 128, keep


def head_probs(q, k, bias):
    s = nt(q, k)
    if bias is not None:
        s = s + bias
    top = jnp.max(s, axis=-1, keepdims=True)
    e = jnp.exp2((s - top) * (SCALE * LOG2E))
    return e * (1.0 / jnp.sum(e, axis=-1, keepdims=True))


def forward_head(load, add, h):
    c, keep = window(h)
    p = head_probs(load(0, c) * keep, load(1, c), None)
    add(0, c, nn(p.astype(BF), load(2, c) * keep))


def backward_head(load, add, h, bias):
    c, keep = window(h)
    q, k, v, g = load(0, c), load(1, c), load(2, c), load(3, c)
    qm, km, gm = q * keep, k * keep, g * keep
    p = head_probs(qm, k, bias)
    pb = p.astype(BF)
    dp = nt(gm, v)
    delta = jnp.sum(dp * p, axis=-1, keepdims=True)
    ds = (p * ((dp - delta) * SCALE)).astype(BF)
    add(2, c, tn(pb, gm))
    add(0, c, nn(ds, km))
    add(1, c, tn(ds, qm))


def columns(j, c):
    return pl.ds(pl.multiple_of(j * D + c, 128), 256)


def adder(ref):
    def add(j, c, value):
        at = columns(j, c)
        ref[:, at] = ref[:, at] + value.astype(BF)

    return add


def flat_loader(qkv_ref, g_ref):
    def load(j, c):
        return qkv_ref[:, columns(j, c)] if j < 3 else g_ref[:, columns(0, c)]

    return load


def block_loader(qkv_ref, g_ref):
    def load(j, c):
        x = qkv_ref[:, :, columns(j, c)] if j < 3 else g_ref[:, :, columns(0, c)]
        return x.reshape(256, 256)

    return load


def spatial_backward_kernel(qkv_ref, g_ref, out_ref):
    out_ref[...] = jnp.zeros_like(out_ref)

    def body(h, carry):
        backward_head(flat_loader(qkv_ref, g_ref), adder(out_ref), h, None)
        return carry

    lax.fori_loop(0, HEADS, body, 0, unroll=4)


def spatial_backward(qkv, grad):
    return pl.pallas_call(
        spatial_backward_kernel,
        out_shape=jax.ShapeDtypeStruct((256, 3 * D), BF),
        in_specs=[pl.BlockSpec(memory_space=pltpu.VMEM)] * 2,
        out_specs=pl.BlockSpec(memory_space=pltpu.VMEM),
        compiler_params=pltpu.CompilerParams(vmem_limit_bytes=VMEM_LIMIT),
        name="spatial_backward",
    )(qkv, grad)


def position():
    s = lax.axis_index("seq")
    d = lax.axis_index("dp")
    return dict(s=s, d=d, core=s % 2, zlo=(s // 2) % 4, x=s // 8, y=d % 4, zhi=d // 4)


def rcopy(src, dst, ssem, rsem, ps, pd):
    return pltpu.make_async_remote_copy(
        src_ref=src,
        dst_ref=dst,
        send_sem=ssem,
        recv_sem=rsem,
        device_id={"seq": ps, "dp": pd},
        device_id_type=pl.DeviceIdType.MESH,
    )


def greet(ps, pd):
    pl.semaphore_signal(
        pltpu.get_barrier_semaphore(),
        inc=1,
        device_id={"seq": ps, "dp": pd},
        device_id_type=pl.DeviceIdType.MESH,
    )


def a2a_start(p, pairs, ssems, rsems):
    def body(k, carry):
        peer = (p["s"] + k) % SEQ
        for i, (src, dst) in enumerate(pairs):
            rcopy(src.at[peer], dst.at[p["s"]], ssems.at[i], rsems.at[i], peer, p["d"]).start()
        return carry

    lax.fori_loop(1, SEQ, body, 0)


def a2a_wait(p, pairs, ssems, rsems):
    for i, (src, dst) in enumerate(pairs):
        part = pl.ds(0, SEQ - 1)
        rcopy(
            src.at[part], dst.at[part], ssems.at[i], rsems.at[i], (p["s"] + 1) % SEQ, p["d"]
        ).wait()


def greet_seq(p):
    def body(k, carry):
        greet((p["s"] + k) % SEQ, p["d"])
        return carry

    lax.fori_loop(1, SEQ, body, 0)


SPLIT = 2048
WA, WB = SPLIT // 4, (4 * D - SPLIT) // 4


def gather_kernel(
    w_ref,
    qkv_ref,
    g_ref,
    spatial_ref,
    wall_ref,
    attended_ref,
    gqkv_ref,
    qkvm_ref,
    gm_ref,
    bias_ref,
    lsem,
    asend,
    arecv,
    wsend,
    wrecv,
):
    p = position()
    s, d, x, y, core, zhi = p["s"], p["d"], p["x"], p["y"], p["core"], p["zhi"]
    own = [
        pltpu.make_async_copy(w_ref, wall_ref.at[d], lsem.at[0]),
        pltpu.make_async_copy(qkv_ref.at[s], qkvm_ref.at[s], lsem.at[1]),
        pltpu.make_async_copy(g_ref.at[s], gm_ref.at[s], lsem.at[2]),
    ]
    for c in own:
        c.start()
    greet_seq(p)
    far = (d + 4) % DP
    greet(s, far)
    y_to = [zhi * 4 + (y + k) % 4 for k in (1, 2, 3)]
    y_from = [zhi * 4 + (y + 4 - k) % 4 for k in (1, 2, 3)]
    y_far = [(1 - zhi) * 4 + (y + 4 - k) % 4 for k in (1, 2, 3)]
    x_to = [((x + k) % 4) * 8 + s % 8 for k in (1, 2, 3)]
    x_from = [(x + 4 - k) % 4 for k in (1, 2, 3)]
    sibling = s + 1 - 2 * core
    for peer in y_to:
        greet(s, peer)
    pl.semaphore_wait(pltpu.get_barrier_semaphore(), SEQ - 1 + 4)

    rows = pl.ds(core * 9, 9)
    other_rows = pl.ds((1 - core) * 9, 9)

    def col_a(xx):
        return pl.ds(pl.multiple_of(xx * WA, 128), WA)

    def col_b(xx):
        return pl.ds(pl.multiple_of(SPLIT + xx * WB, 128), WB)

    all_b = pl.ds(SPLIT, 4 * WB)
    sent = []
    expected = []

    def send(dd, cols, sem, ps, pd, mine=False):
        dst = wall_ref.at[dd, rows, :, cols]
        src = w_ref.at[rows, :, cols] if mine else dst
        c = rcopy(src, dst, wsend.at[sem], wrecv.at[sem], ps, pd)
        c.start()
        sent.append(c)

    def arrived(dd, cols, sem, which=None):
        ref = wall_ref.at[dd, rows if which is None else which, :, cols]
        rcopy(ref, ref, wsend.at[sem], wrecv.at[sem], s, far).wait_recv()

    def hand_on(dd, cols, sem):
        send(dd, cols, sem, sibling, d)
        expected.append((dd, cols, sem))

    send(d, col_b(x), 56, s, far, True)
    send(d, col_a(x), 0, s, far, True)
    for k in range(3):
        send(d, col_a(x), 1 + k, s, y_to[k], True)
    for k in range(3):
        send(d, all_b, 60 + k, s, y_to[k], True)
    pairs = [(qkv_ref, qkvm_ref), (g_ref, gm_ref)]
    a2a_start(p, pairs, asend, arecv)

    arrived(far, col_b(x), 56)
    for k in range(3):
        send(far, col_b(x), 57 + k, x_to[k], d)
    arrived(far, col_a(x), 0)
    for k in range(3):
        send(far, col_a(x), 4 + k, s, y_to[k])
    hand_on(far, col_b(x), 66)

    attended_ref[...] = jnp.zeros_like(attended_ref)

    def spatial(h, carry):
        forward_head(flat_loader(spatial_ref, None), adder(attended_ref), h)
        return carry

    lax.fori_loop(0, HEADS, spatial, 0, unroll=2)

    for k in range(3):
        arrived(far, col_b(x_from[k]), 57 + k)
    for k in range(3):
        send(far, all_b, 63 + k, s, y_to[k])
    for k in range(3):
        hand_on(far, col_b(x_from[k]), 67 + k)
    sources = [far] + y_from + y_far
    for j, dd in enumerate(sources):
        if j:
            arrived(dd, col_a(x), j)
        for k in range(3):
            send(dd, col_a(x), 7 + j * 3 + k, x_to[k], d)
        hand_on(dd, col_a(x), 28 + j)
    for k in range(3):
        arrived(y_from[k], all_b, 60 + k)
        hand_on(y_from[k], all_b, 70 + k)
    for j, dd in enumerate(sources):
        for k in range(3):
            arrived(dd, col_a(x_from[k]), 7 + j * 3 + k)
            hand_on(dd, col_a(x_from[k]), 35 + j * 3 + k)
    for k in range(3):
        arrived(y_far[k], all_b, 63 + k)
        hand_on(y_far[k], all_b, 73 + k)

    at = lax.broadcasted_iota(jnp.int32, (256, 256), 0) % 8
    to = lax.broadcasted_iota(jnp.int32, (256, 256), 1) % 8
    bias_ref[...] = jnp.where(at == to, 0.0, -1e30)
    gqkv_ref[...] = jnp.zeros_like(gqkv_ref)
    a2a_wait(p, pairs, asend, arecv)
    own[1].wait()
    own[2].wait()

    def temporal(h, carry):
        backward_head(block_loader(qkvm_ref, gm_ref), adder(gqkv_ref), h, bias_ref[...])
        return carry

    lax.fori_loop(0, HEADS, temporal, 0, unroll=2)

    for dd, cols, sem in expected:
        arrived(dd, cols, sem, other_rows)
    for c in sent:
        c.wait_send()
    own[0].wait()


def gather_call(w_own, qkv, grad, spatial):
    any_space = pl.BlockSpec(memory_space=pl.ANY)
    vmem = pl.BlockSpec(memory_space=pltpu.VMEM)
    return pl.pallas_call(
        gather_kernel,
        out_shape=(
            jax.ShapeDtypeStruct((DP, 18, 8, 4 * D), BF),
            jax.ShapeDtypeStruct((256, D), BF),
            jax.ShapeDtypeStruct((256, 3 * D), BF),
        ),
        in_specs=[any_space] * 3 + [vmem],
        out_specs=[any_space, vmem, vmem],
        scratch_shapes=[
            pltpu.VMEM((SEQ, 8, 3 * D), BF),
            pltpu.VMEM((SEQ, 8, D), BF),
            pltpu.VMEM((256, 256), F32),
            pltpu.SemaphoreType.DMA((3,)),
            pltpu.SemaphoreType.DMA((2,)),
            pltpu.SemaphoreType.DMA((2,)),
            pltpu.SemaphoreType.DMA((76,)),
            pltpu.SemaphoreType.DMA((76,)),
        ],
        compiler_params=pltpu.CompilerParams(
            collective_id=0, has_side_effects=True, vmem_limit_bytes=VMEM_LIMIT
        ),
        name="gather_and_exchange",
    )(w_own, qkv, grad, spatial)


def exchange_kernel(a_ref, b_ref, am_ref, bm_ref, lsem, asend, arecv):
    p = position()
    s = p["s"]
    own = [
        pltpu.make_async_copy(a_ref.at[s], am_ref.at[s], lsem.at[0]),
        pltpu.make_async_copy(b_ref.at[s], bm_ref.at[s], lsem.at[1]),
    ]
    for c in own:
        c.start()
    greet_seq(p)
    pl.semaphore_wait(pltpu.get_barrier_semaphore(), SEQ - 1)
    pairs = [(a_ref, am_ref), (b_ref, bm_ref)]
    a2a_start(p, pairs, asend, arecv)
    a2a_wait(p, pairs, asend, arecv)
    for c in own:
        c.wait()


def exchange_call(a, b):
    return pl.pallas_call(
        exchange_kernel,
        out_shape=(jax.ShapeDtypeStruct(a.shape, BF), jax.ShapeDtypeStruct(b.shape, BF)),
        in_specs=[pl.BlockSpec(memory_space=pl.ANY)] * 2,
        out_specs=[pl.BlockSpec(memory_space=pl.ANY)] * 2,
        scratch_shapes=[
            pltpu.SemaphoreType.DMA((2,)),
            pltpu.SemaphoreType.DMA((2,)),
            pltpu.SemaphoreType.DMA((2,)),
        ],
        compiler_params=pltpu.CompilerParams(collective_id=1, has_side_effects=True),
        name="exchange",
    )(a, b)


ROWS = 144
QX, OX = 8 * 128, 3 * 128
CZ = 256


def x_start(xx):
    q = xx * 27 // 4
    return q - xx // 3, xx * 2


def z_start(ss):
    xx = ss // 8
    q0, o0 = x_start(xx)
    q = ss * 27 // 32
    q = q - ss // 31
    o = ss * 9 // 32
    o = jnp.minimum(o, o0 + 1)
    return q - q0, o - o0


def reduce_kernel(
    p_ref,
    out_ref,
    mine,
    from_core,
    from_y,
    xq,
    xo,
    zq,
    zo,
    lsem,
    csend,
    crecv,
    ysend,
    yrecv,
    xsend,
    xrecv,
    zsend,
    zrecv,
):
    p = position()
    s, d, x, y, core, zhi, zlo = p["s"], p["d"], p["x"], p["y"], p["core"], p["zhi"], p["zlo"]
    sibling = s + 1 - 2 * core
    z_me = zhi * 4 + zlo
    order = [(y + k) % 4 for k in (1, 2, 3, 0)]
    loads = []
    for i, r in enumerate(order):
        c = pltpu.make_async_copy(p_ref.at[core * 4 + r], mine.at[r], lsem.at[i])
        c.start()
        loads.append(c)
    for z in range(8):
        for c in range(2):
            ps = x * 8 + (z % 4) * 2 + c
            pd = (z // 4) * 4 + y

            @pl.when(jnp.logical_or(ps != s, pd != d))
            def _():
                greet(ps, pd)

    for k in (1, 2, 3):
        greet(s, zhi * 4 + (y + k) % 4)
        greet(((x + k) % 4) * 8 + s % 8, d)
    pl.semaphore_wait(pltpu.get_barrier_semaphore(), 21)

    sent = []

    def send(src, dst, ssem, rsem, ps, pd):
        c = rcopy(src, dst, ssem, rsem, ps, pd)
        c.start()
        sent.append(c)
        return c

    core_copies = []
    for i, r in enumerate(order):
        core_copies.append(
            send(
                p_ref.at[(1 - core) * 4 + r], from_core.at[r], csend.at[i], crecv.at[i], sibling, d
            )
        )
    for i, r in enumerate(order):
        loads[i].wait()
        core_copies[i].wait_recv()

        @pl.loop(0, 9)
        def _(t):
            cols = pl.ds(pl.multiple_of(t * 512, 512), 512)
            mine[r, :, cols] = (
                mine[r, :, cols].astype(F32) + from_core[r, :, cols].astype(F32)
            ).astype(BF)

        if i < 3:
            send(
                mine.at[r], from_y.at[i], ysend.at[i], yrecv.at[i], s, zhi * 4 + (y + i + 1) % 4
            )
    for i in range(3):
        rcopy(from_y.at[i], from_y.at[i], ysend.at[i], yrecv.at[i], sibling, d).wait_recv()

    @pl.loop(0, 9)
    def _(t):
        cols = pl.ds(pl.multiple_of(t * 512, 512), 512)
        total = mine[y, :, cols].astype(F32)
        for i in range(3):
            total = total + from_y[i, :, cols].astype(F32)
        mine[y, :, cols] = total.astype(BF)

    def share(xx):
        q0, o0 = x_start(xx)
        return (
            pl.ds(pl.multiple_of((q0 + 9) * 128, 128), QX),
            pl.ds(pl.multiple_of(o0 * 128, 128), OX),
        )

    for k in (1, 2, 3):
        xx = (x + k) % 4
        qc, oc = share(xx)
        ps = xx * 8 + s % 8
        send(mine.at[y, :, qc], xq.at[k - 1], xsend.at[k - 1], xrecv.at[k - 1], ps, d)
        send(mine.at[y, :, oc], xo.at[k - 1], xsend.at[k + 2], xrecv.at[k + 2], ps, d)
    for k in range(3):
        rcopy(xq.at[k], xq.at[k], xsend.at[k], xrecv.at[k], sibling, d).wait_recv()
        rcopy(xo.at[k], xo.at[k], xsend.at[k + 3], xrecv.at[k + 3], sibling, d).wait_recv()
    qc, oc = share(x)
    xq[3] = (
        (mine[y, :, qc].astype(F32) + xq[0].astype(F32)) + (xq[1].astype(F32) + xq[2].astype(F32))
    ).astype(BF)
    xo[3] = (
        (mine[y, :, oc].astype(F32) + xo[0].astype(F32)) + (xo[1].astype(F32) + xo[2].astype(F32))
    ).astype(BF)

    def z_copies(z2, c2):
        ss = x * 8 + z2 * 2 + c2
        q, o = z_start(ss)
        i = z2 * 2 + c2
        qs = xq.at[3, :, pl.ds(pl.multiple_of(q * 128, 128), CZ)]
        os = xo.at[3, :, pl.ds(pl.multiple_of(o * 128, 128), CZ)]
        return ss, i, qs, os

    for z2 in range(4):
        for c2 in range(2):
            ss, i, qs, os = z_copies(z2, c2)
            pd = core * 4 + y
            is_me = jnp.logical_and(ss == s, pd == d)

            @pl.when(jnp.logical_not(is_me))
            def _():
                rcopy(qs, zq.at[z_me], zsend.at[i], zrecv.at[z_me], ss, pd).start()
                rcopy(os, zo.at[z_me], zsend.at[i + 8], zrecv.at[z_me + 8], ss, pd).start()

            @pl.when(is_me)
            def _():
                pltpu.make_async_copy(qs, zq.at[z_me], zrecv.at[z_me]).start()
                pltpu.make_async_copy(os, zo.at[z_me], zrecv.at[z_me + 8]).start()

    for z in range(8):
        pltpu.make_async_copy(zq.at[z], zq.at[z], zrecv.at[z]).wait()
        pltpu.make_async_copy(zo.at[z], zo.at[z], zrecv.at[z + 8]).wait()
    total_q = zq[0].astype(F32)
    total_o = zo[0].astype(F32)
    for z in range(1, 8):
        total_q = total_q + zq[z].astype(F32)
        total_o = total_o + zo[z].astype(F32)
    out_ref[:, :CZ] = total_q
    out_ref[:, CZ:] = total_o
    for c in sent:
        c.wait_send()
    for z2 in range(4):
        for c2 in range(2):
            ss, i, qs, os = z_copies(z2, c2)
            pd = core * 4 + y

            @pl.when(jnp.logical_or(ss != s, pd != d))
            def _():
                rcopy(qs, zq.at[z_me], zsend.at[i], zrecv.at[z_me], ss, pd).wait_send()
                rcopy(os, zo.at[z_me], zsend.at[i + 8], zrecv.at[z_me + 8], ss, pd).wait_send()


def reduce_call(partial):
    return pl.pallas_call(
        reduce_kernel,
        out_shape=jax.ShapeDtypeStruct((ROWS, 2 * CZ), F32),
        in_specs=[pl.BlockSpec(memory_space=pl.ANY)],
        out_specs=pl.BlockSpec(memory_space=pltpu.VMEM),
        scratch_shapes=[
            pltpu.VMEM((4, ROWS, 4 * D), BF),
            pltpu.VMEM((4, ROWS, 4 * D), BF),
            pltpu.VMEM((3, ROWS, 4 * D), BF),
            pltpu.VMEM((4, ROWS, QX), BF),
            pltpu.VMEM((4, ROWS, OX), BF),
            pltpu.VMEM((8, ROWS, CZ), BF),
            pltpu.VMEM((8, ROWS, CZ), BF),
            pltpu.SemaphoreType.DMA((4,)),
            pltpu.SemaphoreType.DMA((4,)),
            pltpu.SemaphoreType.DMA((4,)),
            pltpu.SemaphoreType.DMA((3,)),
            pltpu.SemaphoreType.DMA((3,)),
            pltpu.SemaphoreType.DMA((6,)),
            pltpu.SemaphoreType.DMA((6,)),
            pltpu.SemaphoreType.DMA((16,)),
            pltpu.SemaphoreType.DMA((16,)),
        ],
        compiler_params=pltpu.CompilerParams(
            collective_id=2, has_side_effects=True, vmem_limit_bytes=VMEM_LIMIT
        ),
        name="reduce_weight_gradients",
    )(partial)


def per_device(
    hidden_in,
    qkv_spatial,
    qkv_temporal,
    grad_out,
    grad_temporal,
    gate_spatial,
    modulation,
    w_out_spatial,
    w_qkv_temporal,
):
    token_rows = 256
    contract_last = (((1,), (1,)), ((), ()))
    contract_rows = (((0,), (0,)), ((), ()))
    w_own = jnp.concatenate([w_out_spatial, w_qkv_temporal], axis=1).reshape(18, 8, 4 * D)
    frame_rows = qkv_spatial.reshape(token_rows, 3 * D)
    w_all, attended_flat, grad_qkv_moved = gather_call(
        w_own,
        qkv_temporal.reshape(SEQ, 8, 3 * D),
        grad_temporal.reshape(SEQ, 8, D),
        frame_rows,
    )
    w_all = w_all.reshape(D, 4 * D)
    w_out_all = w_all[:, :D]
    w_qkv_all = w_all[:, D:]

    projected = jnp.dot(attended_flat, w_out_all, preferred_element_type=F32)
    gate_row = gate_spatial.astype(F32)
    residual = hidden_in.reshape(token_rows, D).astype(F32) + gate_row * projected
    centered = residual - jnp.mean(residual, axis=-1, keepdims=True)
    inv_std = lax.rsqrt(jnp.mean(centered * centered, axis=-1, keepdims=True) + EPSILON)
    unit = centered * inv_std
    shift_row = modulation[:, 0].astype(F32)
    scale_row = modulation[:, 1].astype(F32)
    normed = (unit * (1.0 + scale_row) + shift_row).astype(BF)

    grad_normed_moved = lax.dot_general(
        grad_qkv_moved, w_qkv_all, contract_last, preferred_element_type=F32
    ).astype(BF)
    normed_moved, grad_normed = exchange_call(
        normed.reshape(SEQ, 8, D), grad_normed_moved.reshape(SEQ, 8, D)
    )
    grad_normed = grad_normed.reshape(token_rows, D)

    grad_hat = grad_normed.astype(F32) * (1.0 + scale_row)
    grad_resid = grad_out.reshape(token_rows, D).astype(F32) + inv_std * (
        grad_hat
        - jnp.mean(grad_hat, axis=-1, keepdims=True)
        - unit * jnp.mean(grad_hat * unit, axis=-1, keepdims=True)
    )
    grad_proj = (gate_row * grad_resid).astype(BF)
    grad_attended = lax.dot_general(
        grad_proj, w_out_all, contract_last, preferred_element_type=F32
    ).astype(BF)
    grad_qkv_s = spatial_backward(frame_rows, grad_attended).reshape(qkv_spatial.shape)
    grad_scale = 1.0 / math.sqrt(DP * SEQ * token_rows)
    first = lax.dot_general(attended_flat, grad_proj, contract_rows, preferred_element_type=F32)
    second = lax.dot_general(
        normed_moved.reshape(token_rows, D),
        grad_qkv_moved,
        contract_rows,
        preferred_element_type=F32,
    )
    partial = (jnp.concatenate([first, second], axis=1) * grad_scale).astype(BF)
    sums = reduce_call(partial.reshape(DP, ROWS, 4 * D))
    s = lax.axis_index("seq")
    q_at, o_at = z_start(s)
    q0, o0 = x_start(s // 8)
    grad_w_qkv = lax.dynamic_slice(sums, (0, 108 * s - 128 * (q_at + q0)), (ROWS, 108))
    grad_w_out = lax.dynamic_slice(sums, (0, CZ + 36 * s - 128 * (o_at + o0)), (ROWS, 36))
    return (
        grad_resid.astype(BF).reshape(hidden_in.shape),
        grad_qkv_s,
        grad_w_out,
        grad_w_qkv,
    )


def solution(mesh):
    in_specs = (
        P("dp", "seq", None, None),
        P("dp", "seq", None, None),
        P("dp", "seq", None, None),
        P("dp", "seq", None, None),
        P("dp", "seq", None, None),
        P("dp", None),
        P("dp", None, None),
        P("dp", None),
        P("dp", None),
    )
    out_specs = (
        P("dp", "seq", None, None),
        P("dp", "seq", None, None),
        P("dp", "seq"),
        P("dp", "seq"),
    )
    return jax.shard_map(
        per_device, mesh=mesh, in_specs=in_specs, out_specs=out_specs, check_vma=False
    )
```

profile of v0, /device:TPU:65, one launch (start us, length us, event | category | flops | bytes accessed | tf_op | source)
XLA Modules:
  0.0 284.8 jit_solution(10581789537675295012)
XLA Ops:
  0.6 2.4 maximum_bitcast_fusion.w_ref
  3.1 78.7 %gather_and_exchange.1 = (bf16[8,18,8,4608]{3,2,1,0:T(8,128)(2,1)}, bf16[256,1152]{1,0:T(8,128)(2,1)}, bf16[256,3456]{1,0:T(8,128)(2,1)}) custom-call(bf16[18,8,4608]{2,1,0:T(8,128)(2,1)} %maximum_bitcast_fusion.w_ref, bf16[32,8,3456]{2,1,0:T(8,128)(2,1)} %bitcast.54, bf16[32,8,1152]{2,1,0:T(8,128)(2,1)} %bitcast.56, bf16[256,3456]{1,0:T(8,128)(2,1)} %bitcast.50), custom_call_target="tpu_custom_call" | custom-call | tf_op jit(solution)/shard_map/gather_and_exchange/pallas_call | solution.py:317
  81.8 0.0 copy-start.6
  81.8 3.0 %fusion.25 = (f32[256]{0:T(256)S(1)}, f32[256,1152]{1,0:T(8,128)S(1)}) fusion(bf16[256,1152]{1,0:T(8,128)(2,1)} %get-tuple-element.9, bf16[1152,4608]{1,0:T(8,128)(2,1)} %bitcast.57, f32[1152]{0:T(1024)S(1)} %convert_reduce_fusion.1, bf16[1,1,256,1152]{3,2,1,0:T(8,128)(2,1)S(1)} %copy-done.9), kind=kOutput, calls=%fused_computation.40 | convolution fusion | flops 680656640 | bytes 5019136 | tf_op jit(solution)/shard_map/dot_general | solution.py:610
  84.9 0.3 multiply_reduce_fusion
  85.2 1.1 fusion.22.a_ref
  86.3 0.6 copy-done.1
  86.9 6.7 %fusion.7.b_ref = bf16[32,8,1152]{2,1,0:T(8,128)(2,1)} fusion(bf16[256,3456]{1,0:T(8,128)(2,1)S(1)} %copy-done.1, bf16[1152,4608]{1,0:T(8,128)(2,1)} %bitcast.58), kind=kOutput, calls=%fused_computation.8 | convolution fusion | flops 2038726656 | bytes 10321920 | tf_op jit(solution)/shard_map/dot_general | solution.py:620
  93.5 35.6 %exchange.1 = (bf16[32,8,1152]{2,1,0:T(8,128)(2,1)}, bf16[32,8,1152]{2,1,0:T(8,128)(2,1)}) custom-call(bf16[32,8,1152]{2,1,0:T(8,128)(2,1)} %fusion.22.a_ref, bf16[32,8,1152]{2,1,0:T(8,128)(2,1)} %fusion.7.b_ref), custom_call_target="tpu_custom_call" | custom-call | tf_op jit(solution)/shard_map/exchange/pallas_call | solution.py:362
  129.2 1.5 fusion.20
  130.8 0.6 broadcast_multiply_fusion.1
  131.3 0.2 fusion.21
  131.5 0.7 div.55
  132.2 2.0 convert_bitcast_fusion.1
  134.2 3.6 %convolution_convert_fusion.g_ref = bf16[256,1152]{1,0:T(8,128)(2,1)} fusion(bf16[1152,4608]{1,0:T(8,128)(2,1)} %bitcast.59, f32[256,1152]{1,0:T(8,128)S(1)} %get-tuple-element.25, f32[1152]{0:T(1024)S(1)} %convert_reduce_fusion.1), kind=kOutput, calls=%fused_computation.6 | convolution fusion | flops 680361984 | bytes 4428288 | tf_op jit(solution)/shard_map/dot_general | solution.py:635
  137.8 12.2 %spatial_backward.1 = bf16[256,3456]{1,0:T(8,128)(2,1)} custom-call(bf16[256,3456]{1,0:T(8,128)(2,1)} %bitcast.51, bf16[256,1152]{1,0:T(8,128)(2,1)} %convolution_convert_fusion.g_ref), custom_call_target="tpu_custom_call" | custom-call | tf_op jit(solution)/shard_map/spatial_backward/pallas_call | solution.py:111
  150.0 0.3 copy.15
  150.3 3.9 %fusion.12 = f32[8,144,3456]{2,1,0:T(8,128)S(1)} fusion(bf16[8,144,256]{2,1,0:T(8,128)(2,1)S(1)} %bitcast.52, bf16[256,3456]{1,0:T(8,128)(2,1)} %get-tuple-element.11), kind=kOutput, calls=%fused_computation.11 | convolution fusion | flops 2038431744 | bytes 18284544 | tf_op jit(solution)/shard_map/dot_general | solution.py:641
  154.1 1.0 fusion.23
  155.1 5.0 %fusion.p_ref = bf16[8,144,4608]{2,1,0:T(8,128)(2,1)} fusion(f32[8,144,3456]{2,1,0:T(8,128)S(1)} %fusion.12, f32[8,144,1152]{2,1,0:T(8,128)S(1)} %bitcast.49), kind=kLoop, calls=%fused_computation.1 | loop fusion | flops 15925248 | bytes 31850496 | tf_op jit(solution)/shard_map/convert_element_type | solution.py:647
  160.1 121.3 %reduce_weight_gradients.1 = f32[144,512]{1,0:T(8,128)} custom-call(bf16[8,144,4608]{2,1,0:T(8,128)(2,1)} %fusion.p_ref), custom_call_target="tpu_custom_call" | custom-call | tf_op jit(solution)/shard_map/reduce_weight_gradients/pallas_call | solution.py:554
  281.4 1.0 constant_dynamic-slice_fusion.1
  282.4 0.7 copy.16
  283.1 1.6 constant_dynamic-slice_fusion
  (23 shorter events, 0.1 us)
Async XLA Ops:
  3.1 78.7 %copy-start.8 = (bf16[1,1152]{1,0:T(2,128)(2,1)S(1)}, bf16[1,1152]{1,0:T(2,128)(2,1)}, u32[]{:S(2)}) copy-start(bf16[1,1152]{1,0:T(2,128)(2,1)} %param.14) | copy-start | bytes 6916
  3.1 78.7 %copy-start.9 = (bf16[1,1,256,1152]{3,2,1,0:T(8,128)(2,1)S(1)}, bf16[1,1,256,1152]{3,2,1,0:T(8,128)(2,1)}, u32[]{:S(2)}) copy-start(bf16[1,1,256,1152]{3,2,1,0:T(8,128)(2,1)} %param.9) | copy-start | bytes 1769476
  81.8 3.1 %copy-start.6 = (bf16[1,2,1152]{2,1,0:T(2,128)(2,1)S(1)}, bf16[1,2,1152]{2,1,0:T(2,128)(2,1)}, u32[]{:S(2)}) copy-start(bf16[1,2,1152]{2,1,0:T(2,128)(2,1)} %param.15) | copy-start | bytes 13828
  84.9 44.3 %copy-start.5 = (f32[256]{0:T(256)}, f32[256]{0:T(256)S(1)}, u32[]{:S(2)}) copy-start(f32[256]{0:T(256)S(1)} %broadcast_multiply_fusion.2) | copy-start | bytes 3076
  85.2 1.7 copy-start.1
  85.2 44.0 %copy-start.7 = (f32[256]{0:T(256)}, f32[256]{0:T(256)S(1)}, u32[]{:S(2)}) copy-start(f32[256]{0:T(256)S(1)} %add_rsqrt_fusion) | copy-start | bytes 3076
  129.2 2.1 copy-start
  129.2 3.0 %copy-start.3 = (bf16[1,1,256,1152]{3,2,1,0:T(8,128)(2,1)S(1)}, bf16[1,1,256,1152]{3,2,1,0:T(8,128)(2,1)}, u32[]{:S(2)}) copy-start(bf16[1,1,256,1152]{3,2,1,0:T(8,128)(2,1)} %param.12) | copy-start | bytes 1769476
  137.8 12.2 %copy-start.4 = (bf16[32,8,1152]{2,1,0:T(8,128)(2,1)S(1)}, bf16[32,8,1152]{2,1,0:T(8,128)(2,1)}, u32[]{:S(2)}) copy-start(bf16[32,8,1152]{2,1,0:T(8,128)(2,1)} %get-tuple-element.13) | copy-start | bytes 1769476
  150.3 3.9 %copy-start.2 = (bf16[256,1152]{1,0:T(8,128)(2,1)S(1)}, bf16[256,1152]{1,0:T(8,128)(2,1)}, u32[]{:S(2)}) copy-start(bf16[256,1152]{1,0:T(8,128)(2,1)} %get-tuple-element.9) | copy-start | bytes 1769476
where the time goes:
time: 286 us; the launch traced here: 285 us
  Pallas kernels  248 us (87%)
  matrix products  18.1 us (6%)
  other arithmetic  13.1 us (5%)
  local copies, waits for them, and re-layouts  4.87 us (2%)
    pallas_call x1, Pallas kernels, reduce_call(): pl.pallas_call(reduce_kernel, out_shape=jax.ShapeDtypeStruct((ROWS, 2 * C...  121 us
    pallas_call x1, Pallas kernels, gather_call(): pl.pallas_call(gather_kernel, out_shape=(jax.ShapeDtypeStruct((DP, 18, 8,...  78.7 us
    pallas_call x1, Pallas kernels, exchange_call(): pl.pallas_call(exchange_kernel, out_shape=(jax.ShapeDtypeStruct(a.shape,...  35.6 us
    pallas_call x1, Pallas kernels, spatial_backward(): pl.pallas_call(spatial_backward_kernel, out_shape=jax.ShapeDtypeStruct((2...  12.2 us
    dot_general x1, matrix products, per_device(): lax.dot_general(grad_qkv_moved, w_qkv_all, contract_last, preferred_eleme...  6.65 us

commit v1 on v0

v1 whole, which is shorter than its diff:
```python
import functools
import math

import jax
import jax.numpy as jnp
from jax import lax
from jax.experimental import pallas as pl
from jax.experimental.pallas import tpu as pltpu
from jax.sharding import PartitionSpec as P

HEADS = 16
D = 1152
SEQ = 32
DP = 8
EPSILON = 1e-06
VMEM_LIMIT = 56 * 1024 * 1024
BF = jnp.bfloat16
F32 = jnp.float32


SCALE = 1.0 / math.sqrt(D // HEADS)
LOG2E = math.log2(math.e)


def nt(a, b):
    return lax.dot_general(a, b, (((1,), (1,)), ((), ())), preferred_element_type=F32)


def tn(a, b):
    return lax.dot_general(a, b, (((0,), (0,)), ((), ())), preferred_element_type=F32)


def nn(a, b):
    return jnp.dot(a, b, preferred_element_type=F32)


def window(h):
    chunk = jnp.minimum(h * 9 // 16, 7)
    lane = lax.broadcasted_iota(jnp.int32, (1, 256), 1) + chunk * 128 - h * 72
    keep = jnp.where(jnp.logical_and(lane >= 0, lane < 72), 1.0, 0.0).astype(BF)
    return chunk * 128, keep


def head_probs(q, k, bias):
    s = nt(q, k)
    if bias is not None:
        s = s + bias
    top = jnp.max(s, axis=-1, keepdims=True)
    e = jnp.exp2((s - top) * (SCALE * LOG2E))
    return e * (1.0 / jnp.sum(e, axis=-1, keepdims=True))


def forward_head(load, add, h):
    c, keep = window(h)
    p = head_probs(load(0, c) * keep, load(1, c), None)
    add(0, c, nn(p.astype(BF), load(2, c) * keep))


def backward_head(load, add, h, bias):
    c, keep = window(h)
    q, k, v, g = load(0, c), load(1, c), load(2, c), load(3, c)
    qm, km, gm = q * keep, k * keep, g * keep
    p = head_probs(qm, k, bias)
    pb = p.astype(BF)
    dp = nt(gm, v)
    delta = jnp.sum(dp * p, axis=-1, keepdims=True)
    ds = (p * ((dp - delta) * SCALE)).astype(BF)
    add(2, c, tn(pb, gm))
    add(0, c, nn(ds, km))
    add(1, c, tn(ds, qm))


def columns(j, c):
    return pl.ds(pl.multiple_of(j * D + c, 128), 256)


def adder(ref):
    def add(j, c, value):
        at = columns(j, c)
        ref[:, at] = ref[:, at] + value.astype(BF)

    return add


def flat_loader(qkv_ref, g_ref):
    def load(j, c):
        return qkv_ref[:, columns(j, c)] if j < 3 else g_ref[:, columns(0, c)]

    return load


def block_loader(qkv_ref, g_ref):
    def load(j, c):
        x = qkv_ref[:, :, columns(j, c)] if j < 3 else g_ref[:, :, columns(0, c)]
        return x.reshape(256, 256)

    return load


def position():
    s = lax.axis_index("seq")
    d = lax.axis_index("dp")
    return dict(s=s, d=d, core=s % 2, zlo=(s // 2) % 4, x=s // 8, y=d % 4, zhi=d // 4)


def rcopy(src, dst, ssem, rsem, ps, pd):
    return pltpu.make_async_remote_copy(
        src_ref=src,
        dst_ref=dst,
        send_sem=ssem,
        recv_sem=rsem,
        device_id={"seq": ps, "dp": pd},
        device_id_type=pl.DeviceIdType.MESH,
    )


def greet(ps, pd):
    pl.semaphore_signal(
        pltpu.get_barrier_semaphore(),
        inc=1,
        device_id={"seq": ps, "dp": pd},
        device_id_type=pl.DeviceIdType.MESH,
    )


def a2a_start(p, pairs, ssems, rsems):
    def body(k, carry):
        peer = (p["s"] + k) % SEQ
        for i, (src, dst) in enumerate(pairs):
            rcopy(src.at[peer], dst.at[p["s"]], ssems.at[i], rsems.at[i], peer, p["d"]).start()
        return carry

    lax.fori_loop(1, SEQ, body, 0)


def a2a_wait(p, pairs, ssems, rsems):
    for i, (src, dst) in enumerate(pairs):
        part = pl.ds(0, SEQ - 1)
        rcopy(
            src.at[part], dst.at[part], ssems.at[i], rsems.at[i], (p["s"] + 1) % SEQ, p["d"]
        ).wait()


def greet_seq(p):
    def body(k, carry):
        greet((p["s"] + k) % SEQ, p["d"])
        return carry

    lax.fori_loop(1, SEQ, body, 0)


SPLIT = 2048
WA, WB = SPLIT // 4, (4 * D - SPLIT) // 4


def gather_kernel(
    w_ref,
    qkv_ref,
    g_ref,
    spatial_ref,
    hidden_ref,
    rows_ref,
    attended_ref,
    gqkv_ref,
    wout_ref,
    unit_ref,
    std_ref,
    normedm_ref,
    gn_ref,
    wall_ref,
    qkvm_ref,
    gm_ref,
    bias_ref,
    normed_ref,
    gnt_ref,
    lsem,
    asend,
    arecv,
    wsend,
    wrecv,
):
    p = position()
    s, d, x, y, core, zhi = p["s"], p["d"], p["x"], p["y"], p["core"], p["zhi"]
    own = [
        pltpu.make_async_copy(w_ref, wall_ref.at[d], lsem.at[0]),
        pltpu.make_async_copy(qkv_ref.at[s], qkvm_ref.at[s], lsem.at[1]),
        pltpu.make_async_copy(g_ref.at[s], gm_ref.at[s], lsem.at[2]),
    ]
    for c in own:
        c.start()
    greet_seq(p)
    far = (d + 4) % DP
    greet(s, far)
    y_to = [zhi * 4 + (y + k) % 4 for k in (1, 2, 3)]
    y_from = [zhi * 4 + (y + 4 - k) % 4 for k in (1, 2, 3)]
    y_far = [(1 - zhi) * 4 + (y + 4 - k) % 4 for k in (1, 2, 3)]
    x_to = [((x + k) % 4) * 8 + s % 8 for k in (1, 2, 3)]
    x_from = [(x + 4 - k) % 4 for k in (1, 2, 3)]
    sibling = s + 1 - 2 * core
    for peer in y_to:
        greet(s, peer)
    pl.semaphore_wait(pltpu.get_barrier_semaphore(), SEQ - 1 + 4)

    rows = pl.ds(core * 9, 9)
    other_rows = pl.ds((1 - core) * 9, 9)

    def col_a(xx):
        return pl.ds(pl.multiple_of(xx * WA, 128), WA)

    def col_b(xx):
        return pl.ds(pl.multiple_of(SPLIT + xx * WB, 128), WB)

    all_b = pl.ds(SPLIT, 4 * WB)
    sent = []
    expected = []

    def send(dd, cols, sem, ps, pd, mine=False):
        dst = wall_ref.at[dd, rows, :, cols]
        src = w_ref.at[rows, :, cols] if mine else dst
        c = rcopy(src, dst, wsend.at[sem], wrecv.at[sem], ps, pd)
        c.start()
        sent.append(c)

    def arrived(dd, cols, sem, which=None):
        ref = wall_ref.at[dd, rows if which is None else which, :, cols]
        rcopy(ref, ref, wsend.at[sem], wrecv.at[sem], s, far).wait_recv()

    def hand_on(dd, cols, sem):
        send(dd, cols, sem, sibling, d)
        expected.append((dd, cols, sem))

    send(d, col_b(x), 56, s, far, True)
    send(d, col_a(x), 0, s, far, True)
    for k in range(3):
        send(d, col_a(x), 1 + k, s, y_to[k], True)
    for k in range(3):
        send(d, all_b, 60 + k, s, y_to[k], True)
    pairs = [(qkv_ref, qkvm_ref), (g_ref, gm_ref)]
    a2a_start(p, pairs, asend, arecv)

    arrived(far, col_b(x), 56)
    for k in range(3):
        send(far, col_b(x), 57 + k, x_to[k], d)
    arrived(far, col_a(x), 0)
    for k in range(3):
        send(far, col_a(x), 4 + k, s, y_to[k])
    hand_on(far, col_b(x), 66)

    attended_ref[...] = jnp.zeros_like(attended_ref)

    def spatial(h, carry):
        forward_head(flat_loader(spatial_ref, None), adder(attended_ref), h)
        return carry

    lax.fori_loop(0, HEADS, spatial, 0, unroll=2)

    for k in range(3):
        arrived(far, col_b(x_from[k]), 57 + k)
    for k in range(3):
        send(far, all_b, 63 + k, s, y_to[k])
    for k in range(3):
        hand_on(far, col_b(x_from[k]), 67 + k)
    sources = [far] + y_from + y_far
    for j, dd in enumerate(sources):
        if j:
            arrived(dd, col_a(x), j)
        for k in range(3):
            send(dd, col_a(x), 7 + j * 3 + k, x_to[k], d)
        hand_on(dd, col_a(x), 28 + j)
    for k in range(3):
        arrived(y_from[k], all_b, 60 + k)
        hand_on(y_from[k], all_b, 70 + k)
    for j, dd in enumerate(sources):
        for k in range(3):
            arrived(dd, col_a(x_from[k]), 7 + j * 3 + k)
            hand_on(dd, col_a(x_from[k]), 35 + j * 3 + k)
    for k in range(3):
        arrived(y_far[k], all_b, 63 + k)
        hand_on(y_far[k], all_b, 73 + k)

    at = lax.broadcasted_iota(jnp.int32, (256, 256), 0) % 8
    to = lax.broadcasted_iota(jnp.int32, (256, 256), 1) % 8
    bias_ref[...] = jnp.where(at == to, 0.0, -1e30)
    gqkv_ref[...] = jnp.zeros_like(gqkv_ref)

    own[0].wait()
    for dd, cols, sem in expected:
        if sem < 66:
            arrived(dd, cols, sem, other_rows)

    def assemble(dd, carry):
        at = pl.ds(pl.multiple_of(dd * ROWS, 16), ROWS)
        wout_ref[at, :] = wall_ref[dd, :, :, :D].reshape(ROWS, D)
        return carry

    lax.fori_loop(0, DP, assemble, 0)

    def project(t, carry):
        at = pl.ds(pl.multiple_of(t * 384, 128), 384)
        unit_ref[:, at] = hidden_ref[:, at].astype(F32) + rows_ref[0:1, at] * nn(
            attended_ref[...], wout_ref[:, at]
        )
        return carry

    lax.fori_loop(0, 3, project, 0)

    def normalise(t, carry):
        at = pl.ds(pl.multiple_of(t * 32, 32), 32)
        residual = unit_ref[at, :]
        centered = residual - jnp.mean(residual, axis=-1, keepdims=True)
        inv_std = lax.rsqrt(jnp.mean(centered * centered, axis=-1, keepdims=True) + EPSILON)
        unit = centered * inv_std
        unit_ref[at, :] = unit
        std_ref[at, :] = jnp.broadcast_to(inv_std, (32, 128))
        normed = unit * (1.0 + rows_ref[2:3, :]) + rows_ref[1:2, :]
        normed_ref[pl.ds(t * 4, 4)] = normed.reshape(4, 8, D).astype(BF)
        return carry

    lax.fori_loop(0, 8, normalise, 0)
    own_normed = pltpu.make_async_copy(normed_ref.at[s], normedm_ref.at[s], lsem.at[3])
    own_normed.start()
    normed_pair = [(normed_ref, normedm_ref)]
    a2a_start(p, normed_pair, asend.at[pl.ds(2, 1)], arecv.at[pl.ds(2, 1)])

    a2a_wait(p, pairs, asend, arecv)
    own[1].wait()
    own[2].wait()

    def temporal(h, carry):
        backward_head(block_loader(qkvm_ref, gm_ref), adder(gqkv_ref), h, bias_ref[...])
        return carry

    lax.fori_loop(0, HEADS, temporal, 0, unroll=2)

    for dd, cols, sem in expected:
        if sem >= 66:
            arrived(dd, cols, sem, other_rows)

    def back_project(dd, carry):
        at = pl.ds(pl.multiple_of(dd * ROWS, 16), ROWS)
        gnt_ref[at, :] = nt(wall_ref[dd, :, :, D:].reshape(ROWS, 3 * D), gqkv_ref[...])
        return carry

    lax.fori_loop(0, DP, back_project, 0)

    def turn(t, carry):
        at = pl.ds(pl.multiple_of(t * 128, 128), 128)
        gn_ref[:, :, at] = gnt_ref[at, :].T.reshape(SEQ, 8, 128).astype(BF)
        return carry

    lax.fori_loop(0, 9, turn, 0)
    a2a_wait(p, normed_pair, asend.at[pl.ds(2, 1)], arecv.at[pl.ds(2, 1)])
    own_normed.wait()
    for c in sent:
        c.wait_send()


def gather_call(w_own, qkv, grad, spatial, hidden, rows):
    any_space = pl.BlockSpec(memory_space=pl.ANY)
    vmem = pl.BlockSpec(memory_space=pltpu.VMEM)
    return pl.pallas_call(
        gather_kernel,
        out_shape=(
            jax.ShapeDtypeStruct((256, D), BF),
            jax.ShapeDtypeStruct((256, 3 * D), BF),
            jax.ShapeDtypeStruct((D, D), BF),
            jax.ShapeDtypeStruct((256, D), F32),
            jax.ShapeDtypeStruct((256, 128), F32),
            jax.ShapeDtypeStruct((SEQ, 8, D), BF),
            jax.ShapeDtypeStruct((SEQ, 8, D), BF),
        ),
        in_specs=[any_space] * 3 + [vmem] * 3,
        out_specs=[vmem] * 5 + [any_space, vmem],
        scratch_shapes=[
            pltpu.VMEM((DP, 18, 8, 4 * D), BF),
            pltpu.VMEM((SEQ, 8, 3 * D), BF),
            pltpu.VMEM((SEQ, 8, D), BF),
            pltpu.VMEM((256, 256), F32),
            pltpu.VMEM((SEQ, 8, D), BF),
            pltpu.VMEM((D, 256), F32),
            pltpu.SemaphoreType.DMA((4,)),
            pltpu.SemaphoreType.DMA((3,)),
            pltpu.SemaphoreType.DMA((3,)),
            pltpu.SemaphoreType.DMA((76,)),
            pltpu.SemaphoreType.DMA((76,)),
        ],
        compiler_params=pltpu.CompilerParams(
            collective_id=0, has_side_effects=True, vmem_limit_bytes=VMEM_LIMIT
        ),
        name="gather_and_exchange",
    )(w_own, qkv, grad, spatial, hidden, rows)


ROWS = 144
QX, OX = 8 * 128, 3 * 128
CZ = 256


def x_start(xx):
    q = xx * 27 // 4
    return q - xx // 3, xx * 2


def z_start(ss):
    xx = ss // 8
    q0, o0 = x_start(xx)
    q = ss * 27 // 32
    q = q - ss // 31
    o = ss * 9 // 32
    o = jnp.minimum(o, o0 + 1)
    return q - q0, o - o0


class Reducer:
    def __init__(self, p, which, width, cover, bufs, sems):
        self.p, self.which, self.width, self.cover = p, which, width, cover
        self.lhs_t, self.to_core, self.mine, self.from_core, self.b1y, self.b1x = bufs[:6]
        self.part, self.b2, self.total, self.zbuf = bufs[6:]
        self.csend, self.crecv, self.s1send, self.s1recv = sems[:4]
        self.s2send, self.s2recv, self.zsend, self.zrecv = sems[4:]
        y, x, s = p["y"], p["x"], p["s"]
        self.order = [(y + k) % 4 for k in (1, 2, 3, 0)]
        self.y_to = [p["zhi"] * 4 + r for r in self.order[:3]]
        self.xs = [(x + k) % 4 for k in (1, 2, 3)]
        self.x_to = [xx * 8 + s % 8 for xx in self.xs]

    def cols(self, xx, t=0, size=None):
        first = x_start(xx)[self.which] * 128
        return pl.ds(pl.multiple_of(first + t, 128), self.cover if size is None else size)

    def core_copy(self, i):
        r = self.order[i]
        p = self.p
        return rcopy(
            self.to_core.at[r],
            self.from_core.at[r],
            self.csend.at[i],
            self.crecv.at[i],
            p["s"] + 1 - 2 * p["core"],
            p["d"],
        )

    def first_y(self, i):
        return rcopy(
            self.mine.at[self.order[i]],
            self.b1y.at[i],
            self.s1send.at[i],
            self.s1recv.at[i],
            self.p["s"],
            self.y_to[i],
        )

    def first_x(self, k, i):
        r = self.order[i]
        return rcopy(
            self.mine.at[r, :, self.cols(self.xs[k])],
            self.b1x.at[k, r],
            self.s1send.at[k * 4 + i],
            self.s1recv.at[k * 4 + i],
            self.x_to[k],
            self.p["d"],
        )

    def second_x(self, k):
        return rcopy(
            self.mine.at[self.p["y"], :, self.cols(self.xs[k])],
            self.b2.at[k],
            self.s2send.at[k],
            self.s2recv.at[k],
            self.x_to[k],
            self.p["d"],
        )

    def second_y(self, i):
        return rcopy(
            self.part.at[self.order[i]],
            self.b2.at[i],
            self.s2send.at[i],
            self.s2recv.at[i],
            self.p["s"],
            self.y_to[i],
        )

    def z_target(self, i):
        p = self.p
        ss = p["x"] * 8 + i
        pd = p["core"] * 4 + p["y"]
        at = z_start(ss)[self.which]
        src = self.total.at[:, pl.ds(pl.multiple_of(at * 128, 128), CZ)]
        z_me = p["zhi"] * 4 + p["zlo"]
        return ss, pd, src, z_me

    def z_copy(self, i):
        ss, pd, src, z_me = self.z_target(i)
        return rcopy(src, self.zbuf.at[z_me], self.zsend.at[i], self.zrecv.at[z_me], ss, pd)

    def z_local(self, i):
        ss, pd, src, z_me = self.z_target(i)
        return pltpu.make_async_copy(src, self.zbuf.at[z_me], self.zrecv.at[z_me])

    def product(self, block, rhs_ref, dst, r, add):
        lhs = self.lhs_t[pl.ds(pl.multiple_of(block * ROWS, 16), ROWS), :]
        step = self.width // 9

        def body(t, carry):
            at = pl.ds(pl.multiple_of(t * step, 128), step)
            value = nn(lhs, rhs_ref[:, at]) * GRAD_SCALE
            if add is not None:
                value = value + add[r, :, at].astype(F32)
            dst[r, :, at] = value.astype(BF)
            return carry

        lax.fori_loop(0, 9, body, 0)

    def start(self, load_lhs, rhs_ref):
        def turn(t, carry):
            at = pl.ds(pl.multiple_of(t * 128, 128), 128)
            self.lhs_t[at, :] = load_lhs(at).T
            return carry

        lax.fori_loop(0, 9, turn, 0)
        for i, r in enumerate(self.order):
            self.product((1 - self.p["core"]) * 4 + r, rhs_ref, self.to_core, r, None)
            self.core_copy(i).start()

    def first(self, rhs_ref):
        core = self.p["core"]
        for i, r in enumerate(self.order):
            self.core_copy(i).wait_recv()
            self.product(core * 4 + r, rhs_ref, self.mine, r, self.from_core)

            if i < 3:

                @pl.when(core == 0)
                def _():
                    self.first_y(i).start()

            @pl.when(core == 1)
            def _():
                for k in range(3):
                    self.first_x(k, i).start()

    def second(self):
        p = self.p
        y = p["y"]

        @pl.when(p["core"] == 0)
        def _():
            for i in range(3):
                self.first_y(i).wait_recv()
            step = self.width // 9

            def body(t, carry):
                at = pl.ds(pl.multiple_of(t * step, 128), step)
                total = self.mine[y, :, at].astype(F32)
                for i in range(3):
                    total = total + self.b1y[i, :, at].astype(F32)
                self.mine[y, :, at] = total.astype(BF)
                return carry

            lax.fori_loop(0, 9, body, 0)
            for k in range(3):
                self.second_x(k).start()

        @pl.when(p["core"] == 1)
        def _():
            for i, r in enumerate(self.order):
                for k in range(3):
                    self.first_x(k, i).wait_recv()

                def body(t, carry):
                    at = pl.ds(pl.multiple_of(t * 128, 128), 128)
                    total = self.mine[r, :, self.cols(p["x"], t * 128, 128)].astype(F32)
                    for k in range(3):
                        total = total + self.b1x[k, r, :, at].astype(F32)
                    self.part[r, :, at] = total.astype(BF)
                    return carry

                lax.fori_loop(0, self.cover // 128, body, 0)
                if i < 3:
                    self.second_y(i).start()

    def third(self):
        p = self.p
        y, x, core = p["y"], p["x"], p["core"]

        def finish(load):
            def body(t, carry):
                at = pl.ds(pl.multiple_of(t * 128, 128), 128)
                total = load(t).astype(F32)
                for k in range(3):
                    total = total + self.b2[k, :, at].astype(F32)
                self.total[:, at] = total.astype(BF)
                return carry

            lax.fori_loop(0, self.cover // 128, body, 0)

        @pl.when(core == 0)
        def _():
            for k in range(3):
                self.second_x(k).wait_recv()
            finish(lambda t: self.mine[y, :, self.cols(x, t * 128, 128)])

        @pl.when(core == 1)
        def _():
            for i in range(3):
                self.second_y(i).wait_recv()
            finish(lambda t: self.part[y, :, pl.ds(pl.multiple_of(t * 128, 128), 128)])

        for i in range(8):
            ss, pd, _, _ = self.z_target(i)
            is_me = jnp.logical_and(ss == p["s"], pd == p["d"])

            @pl.when(jnp.logical_not(is_me))
            def _():
                self.z_copy(i).start()

            @pl.when(is_me)
            def _():
                self.z_local(i).start()

    def last(self, out_ref, at):
        for z in range(8):
            pltpu.make_async_copy(self.zbuf.at[z], self.zbuf.at[z], self.zrecv.at[z]).wait()
        total = self.zbuf[0].astype(F32)
        for z in range(1, 8):
            total = total + self.zbuf[z].astype(F32)
        out_ref[:, at : at + CZ] = total

    def drain(self):
        p = self.p
        for i in range(4):
            self.core_copy(i).wait_send()

        @pl.when(p["core"] == 0)
        def _():
            for i in range(3):
                self.first_y(i).wait_send()
                self.second_x(i).wait_send()

        @pl.when(p["core"] == 1)
        def _():
            for k in range(3):
                for i in range(4):
                    self.first_x(k, i).wait_send()
                self.second_y(k).wait_send()

        for i in range(8):
            ss, pd, _, _ = self.z_target(i)

            @pl.when(jnp.logical_or(ss != p["s"], pd != p["d"]))
            def _():
                self.z_copy(i).wait_send()


def reducer_scratch(width, cover):
    bufs = [
        pltpu.VMEM((D, 256), BF),
        pltpu.VMEM((4, ROWS, width), BF),
        pltpu.VMEM((4, ROWS, width), BF),
        pltpu.VMEM((4, ROWS, width), BF),
        pltpu.VMEM((3, ROWS, width), BF),
        pltpu.VMEM((3, 4, ROWS, cover), BF),
        pltpu.VMEM((4, ROWS, cover), BF),
        pltpu.VMEM((3, ROWS, cover), BF),
        pltpu.VMEM((ROWS, cover), BF),
        pltpu.VMEM((8, ROWS, CZ), BF),
    ]
    sems = [pltpu.SemaphoreType.DMA((n,)) for n in (4, 4, 12, 12, 3, 3, 8, 8)]
    return bufs + sems


GRAD_SCALE = 1.0 / math.sqrt(DP * SEQ * 256)


def reduce_kernel(
    gn_ref,
    normedm_ref,
    gqkv_ref,
    wout_ref,
    attended_ref,
    spatial_ref,
    unit_ref,
    std_ref,
    gout_ref,
    rows_ref,
    hidden_out,
    spatial_out,
    sums_out,
    *scratch,
):
    p = position()
    s, d, x, y, zhi = p["s"], p["d"], p["x"], p["y"], p["zhi"]
    rq = Reducer(p, 0, 3 * D, QX, scratch[0:10], scratch[10:18])
    ro = Reducer(p, 1, D, OX, scratch[18:28], scratch[28:36])
    gnm_ref, proj_ref, gatt_ref, lsem, asend, arecv = scratch[36:]
    own = pltpu.make_async_copy(gn_ref.at[s], gnm_ref.at[s], lsem)
    own.start()
    greet_seq(p)
    for k in (1, 2, 3):
        greet(s, zhi * 4 + (y + k) % 4)
    for i in range(8):
        greet(x * 8 + i, (1 - zhi) * 4 + y)
    pl.semaphore_wait(pltpu.get_barrier_semaphore(), SEQ - 1 + 3 + 8)

    pairs = [(gn_ref, gnm_ref)]
    a2a_start(p, pairs, asend, arecv)
    rq.start(lambda at: normedm_ref[:, :, at].reshape(256, 128), gqkv_ref)
    rq.first(gqkv_ref)

    a2a_wait(p, pairs, asend, arecv)
    own.wait()

    def norm_backward(t, carry):
        at = pl.ds(pl.multiple_of(t * 32, 32), 32)
        unit = unit_ref[at, :]
        inv_std = std_ref[at, 0:1]
        grad_normed = gnm_ref[pl.ds(t * 4, 4)].astype(F32).reshape(32, D)
        grad_hat = grad_normed * (1.0 + rows_ref[2:3, :])
        grad_resid = gout_ref[at, :].astype(F32) + inv_std * (
            grad_hat
            - jnp.mean(grad_hat, axis=-1, keepdims=True)
            - unit * jnp.mean(grad_hat * unit, axis=-1, keepdims=True)
        )
        hidden_out[at, :] = grad_resid.astype(BF)
        proj_ref[at, :] = (rows_ref[0:1, :] * grad_resid).astype(BF)
        return carry

    lax.fori_loop(0, 8, norm_backward, 0)
    ro.start(lambda at: attended_ref[:, at], proj_ref)

    def back_project(t, carry):
        at = pl.ds(pl.multiple_of(t * 128, 128), 128)
        gatt_ref[:, at] = nt(proj_ref[...], wout_ref[at, :]).astype(BF)
        return carry

    lax.fori_loop(0, 9, back_project, 0)
    ro.first(proj_ref)
    spatial_out[...] = jnp.zeros_like(spatial_out)

    def spatial(h, carry):
        backward_head(flat_loader(spatial_ref, gatt_ref), adder(spatial_out), h, None)
        return carry

    lax.fori_loop(0, HEADS // 2, spatial, 0, unroll=2)
    rq.second()
    lax.fori_loop(HEADS // 2, HEADS, spatial, 0, unroll=2)
    rq.third()
    ro.second()
    ro.third()
    rq.last(sums_out, 0)
    ro.last(sums_out, CZ)
    rq.drain()
    ro.drain()


def reduce_call(*args):
    any_space = pl.BlockSpec(memory_space=pl.ANY)
    vmem = pl.BlockSpec(memory_space=pltpu.VMEM)
    return pl.pallas_call(
        reduce_kernel,
        out_shape=(
            jax.ShapeDtypeStruct((256, D), BF),
            jax.ShapeDtypeStruct((256, 3 * D), BF),
            jax.ShapeDtypeStruct((ROWS, 2 * CZ), F32),
        ),
        in_specs=[any_space] + [vmem] * 9,
        out_specs=[vmem] * 3,
        scratch_shapes=reducer_scratch(3 * D, QX)
        + reducer_scratch(D, OX)
        + [
            pltpu.VMEM((SEQ, 8, D), BF),
            pltpu.VMEM((256, D), BF),
            pltpu.VMEM((256, D), BF),
            pltpu.SemaphoreType.DMA,
            pltpu.SemaphoreType.DMA((1,)),
            pltpu.SemaphoreType.DMA((1,)),
        ],
        compiler_params=pltpu.CompilerParams(
            collective_id=1, has_side_effects=True, vmem_limit_bytes=VMEM_LIMIT
        ),
        name="reduce_weight_gradients",
    )(*args)


def per_device(
    hidden_in,
    qkv_spatial,
    qkv_temporal,
    grad_out,
    grad_temporal,
    gate_spatial,
    modulation,
    w_out_spatial,
    w_qkv_temporal,
):
    token_rows = 256
    w_own = jnp.concatenate([w_out_spatial, w_qkv_temporal], axis=1).reshape(18, 8, 4 * D)
    frame_rows = qkv_spatial.reshape(token_rows, 3 * D)
    rows = jnp.concatenate([gate_spatial, modulation[0]], axis=0).astype(F32)
    attended, grad_qkv_moved, w_out, unit, inv_std, normed_moved, grad_normed = gather_call(
        w_own,
        qkv_temporal.reshape(SEQ, 8, 3 * D),
        grad_temporal.reshape(SEQ, 8, D),
        frame_rows,
        hidden_in.reshape(token_rows, D),
        rows,
    )
    grad_hidden, grad_qkv_s, sums = reduce_call(
        grad_normed,
        normed_moved,
        grad_qkv_moved,
        w_out,
        attended,
        frame_rows,
        unit,
        inv_std,
        grad_out.reshape(token_rows, D),
        rows,
    )
    s = lax.axis_index("seq")
    q_at, o_at = z_start(s)
    q0, o0 = x_start(s // 8)
    grad_w_qkv = lax.dynamic_slice(sums, (0, 108 * s - 128 * (q_at + q0)), (ROWS, 108))
    grad_w_out = lax.dynamic_slice(sums, (0, CZ + 36 * s - 128 * (o_at + o0)), (ROWS, 36))
    return (
        grad_hidden.reshape(hidden_in.shape),
        grad_qkv_s.reshape(qkv_spatial.shape),
        grad_w_out,
        grad_w_qkv,
    )


def solution(mesh):
    in_specs = (
        P("dp", "seq", None, None),
        P("dp", "seq", None, None),
        P("dp", "seq", None, None),
        P("dp", "seq", None, None),
        P("dp", "seq", None, None),
        P("dp", None),
        P("dp", None, None),
        P("dp", None),
        P("dp", None),
    )
    out_specs = (
        P("dp", "seq", None, None),
        P("dp", "seq", None, None),
        P("dp", "seq"),
        P("dp", "seq"),
    )
    return jax.shard_map(
        per_device, mesh=mesh, in_specs=in_specs, out_specs=out_specs, check_vma=False
    )
```

time: 286 us -> 203 us (0.71)
  Pallas kernels: 248 us -> 193 us
  matrix products: 18.1 us -> 0 us
  other arithmetic: 13.1 us -> 3.05 us
    pallas_call x4 -> x2, Pallas kernels: 248 us -> 193 us  [the longest x1 98.1 us: reduce_call(): pl.pallas_call(reduce_kernel, out_shape=(jax.ShapeDtypeStruct((256, D), B...]
    dot_general x5 -> x0, matrix products: 18.1 us -> none  [the longest x1 6.65 us: per_device(): lax.dot_general(grad_qkv_moved, w_qkv_all, contract_last, preferred_eleme...]
    convert_element_type x1, other arithmetic: 4.96 us -> 0.62 us  [per_device(): rows = jnp.concatenate([gate_spatial, modulation[0]], axis=0).astype(F32)]
    reshape x2 -> x0, other arithmetic: 3.13 us -> none  [the longest x1 2.04 us: per_device(): grad_resid.astype(BF).reshape(hidden_in.shape)]
where the time goes in v1:
time: 203 us
  Pallas kernels  193 us (95%)
  local copies, waits for them, and re-layouts  6.6 us (3%)
  other arithmetic  3.05 us (2%)
    pallas_call x1, Pallas kernels, reduce_call(): pl.pallas_call(reduce_kernel, out_shape=(jax.ShapeDtypeStruct((256, D), B...  98.1 us
    pallas_call x1, Pallas kernels, gather_call(): pl.pallas_call(gather_kernel, out_shape=(jax.ShapeDtypeStruct((256, D), B...  94.5 us

profile of v1, /device:TPU:65, one launch (start us, length us, event | category | flops | bytes accessed | tf_op | source)
XLA Modules:
  0.0 202.9 jit_solution(17907101193589984861)
XLA Ops:
  0.6 0.0 copy-start.1
  0.6 0.0 copy-start.2
  0.7 2.4 %maximum_bitcast_fusion.w_ref = bf16[18,8,4608]{2,1,0:T(8,128)(2,1)} fusion(bf16[144,3456]{1,0:T(8,128)(2,1)} %param.17, bf16[144,1152]{1,0:T(8,128)(2,1)} %param.16), kind=kLoop, calls=%fused_computation | loop fusion | flops 2654208 | bytes 2654208 | tf_op jit(solution)/shard_map/reshape | solution.py:798
  3.1 0.0 copy-done.1
  3.1 0.0 copy-done.2
  3.1 0.6 maximum_convert_fusion.rows_ref
  3.7 94.5 %gather_and_exchange.1 = (bf16[256,1152]{1,0:T(8,128)(2,1)}, bf16[256,3456]{1,0:T(8,128)(2,1)}, bf16[1152,1152]{1,0:T(8,128)(2,1)}, f32[256,1152]{1,0:T(8,128)},...) custom-call(bf16[18,8,4608]{2,1,0:T(8,128)(2,1)} %maximum_bitcast_fusion.w_ref, ...), custom_call_target="tpu_custom_call" | custom-call | tf_op jit(solution)/shard_map/gather_and_exchange/pallas_call | solution.py:361
  98.2 98.1 %reduce_weight_gradients.1 = (bf16[256,1152]{1,0:T(8,128)(2,1)}, bf16[256,3456]{1,0:T(8,128)(2,1)}, f32[144,512]{1,0:T(8,128)}) custom-call(bf16[32,8,1152]{2,1,0:T(8,128)(2,1)} %get-tuple-element.14.gn_ref, bf16[32,8,1152]{2,1,0:T(8,128)(2,1)} %get-tuple-element.15.normedm_ref, bf16[256,3456]{1,0:T(8,128)(2,1)} %get-tuple-element.16.gqkv_ref, ...), custom_call_target="tpu_custom_call" | custom-call | tf_op jit(solution)/shard_map/reduce_weight_gradients/pallas_call | solution.py:760
  196.3 0.0 copy-start
  196.3 1.1 constant_dynamic-slice_fusion.1
  197.4 0.7 copy.13
  198.1 1.6 constant_dynamic-slice_fusion
  199.8 1.9 copy.16
  201.7 0.0 copy-done
  201.7 1.2 copy.17
Async XLA Ops:
  0.6 2.5 %copy-start.1 = (bf16[1,2,1152]{2,1,0:T(2,128)(2,1)S(1)}, bf16[1,2,1152]{2,1,0:T(2,128)(2,1)}, u32[]{:S(2)}) copy-start(bf16[1,2,1152]{2,1,0:T(2,128)(2,1)} %param.15) | copy-start | bytes 13828
  0.6 2.5 %copy-start.2 = (bf16[1,1152]{1,0:T(2,128)(2,1)S(1)}, bf16[1,1152]{1,0:T(2,128)(2,1)}, u32[]{:S(2)}) copy-start(bf16[1,1152]{1,0:T(2,128)(2,1)} %param.14) | copy-start | bytes 6916
  196.3 5.4 %copy-start = (bf16[256,3456]{1,0:T(8,128)(2,1)S(1)}, bf16[256,3456]{1,0:T(8,128)(2,1)}, u32[]{:S(2)}) copy-start(bf16[256,3456]{1,0:T(8,128)(2,1)} %get-tuple-element.22) | copy-start | bytes 5308420

commit v2 on v1

v2 whole, which is shorter than its diff:
```python
import functools
import math

import jax
import jax.numpy as jnp
from jax import lax
from jax.experimental import pallas as pl
from jax.experimental.pallas import tpu as pltpu
from jax.sharding import PartitionSpec as P

HEADS = 16
D = 1152
SEQ = 32
DP = 8
EPSILON = 1e-06
VMEM_LIMIT = 56 * 1024 * 1024
BF = jnp.bfloat16
F32 = jnp.float32


SCALE = 1.0 / math.sqrt(D // HEADS)
LOG2E = math.log2(math.e)


def nt(a, b):
    return lax.dot_general(a, b, (((1,), (1,)), ((), ())), preferred_element_type=F32)


def tn(a, b):
    return lax.dot_general(a, b, (((0,), (0,)), ((), ())), preferred_element_type=F32)


def nn(a, b):
    return jnp.dot(a, b, preferred_element_type=F32)


def window(h):
    chunk = jnp.minimum(h * 9 // 16, 7)
    lane = lax.broadcasted_iota(jnp.int32, (1, 256), 1) + chunk * 128 - h * 72
    keep = jnp.where(jnp.logical_and(lane >= 0, lane < 72), 1.0, 0.0).astype(BF)
    return chunk * 128, keep


def head_probs(q, k, bias):
    s = nt(q, k)
    if bias is not None:
        s = s + bias
    top = jnp.max(s, axis=-1, keepdims=True)
    e = jnp.exp2((s - top) * (SCALE * LOG2E))
    return e * (1.0 / jnp.sum(e, axis=-1, keepdims=True))


def forward_head(load, add, h):
    c, keep = window(h)
    p = head_probs(load(0, c) * keep, load(1, c), None)
    add(0, c, nn(p.astype(BF), load(2, c) * keep))


def backward_head(load, add, h, bias):
    c, keep = window(h)
    q, k, v, g = load(0, c), load(1, c), load(2, c), load(3, c)
    qm, km, gm = q * keep, k * keep, g * keep
    p = head_probs(qm, k, bias)
    pb = p.astype(BF)
    dp = nt(gm, v)
    delta = jnp.sum(dp * p, axis=-1, keepdims=True)
    ds = (p * ((dp - delta) * SCALE)).astype(BF)
    add(2, c, tn(pb, gm))
    add(0, c, nn(ds, km))
    add(1, c, tn(ds, qm))


def columns(j, c):
    return pl.ds(pl.multiple_of(j * D + c, 128), 256)


def adder(ref):
    def add(j, c, value):
        at = columns(j, c)
        ref[:, at] = ref[:, at] + value.astype(BF)

    return add


def flat_loader(qkv_ref, g_ref):
    def load(j, c):
        return qkv_ref[:, columns(j, c)] if j < 3 else g_ref[:, columns(0, c)]

    return load


def block_loader(qkv_ref, g_ref):
    def load(j, c):
        x = qkv_ref[:, :, columns(j, c)] if j < 3 else g_ref[:, :, columns(0, c)]
        return x.reshape(256, 256)

    return load


def position():
    s = lax.axis_index("seq")
    d = lax.axis_index("dp")
    return dict(s=s, d=d, core=s % 2, zlo=(s // 2) % 4, x=s // 8, y=d % 4, zhi=d // 4)


def rcopy(src, dst, ssem, rsem, ps, pd):
    return pltpu.make_async_remote_copy(
        src_ref=src,
        dst_ref=dst,
        send_sem=ssem,
        recv_sem=rsem,
        device_id={"seq": ps, "dp": pd},
        device_id_type=pl.DeviceIdType.MESH,
    )


def greet(ps, pd):
    pl.semaphore_signal(
        pltpu.get_barrier_semaphore(),
        inc=1,
        device_id={"seq": ps, "dp": pd},
        device_id_type=pl.DeviceIdType.MESH,
    )


def a2a_start(p, pairs, ssems, rsems):
    def body(k, carry):
        peer = (p["s"] + k) % SEQ
        for i, (src, dst) in enumerate(pairs):
            rcopy(src.at[peer], dst.at[p["s"]], ssems.at[i], rsems.at[i], peer, p["d"]).start()
        return carry

    lax.fori_loop(1, SEQ, body, 0)


def a2a_wait(p, pairs, ssems, rsems):
    for i, (src, dst) in enumerate(pairs):
        part = pl.ds(0, SEQ - 1)
        rcopy(
            src.at[part], dst.at[part], ssems.at[i], rsems.at[i], (p["s"] + 1) % SEQ, p["d"]
        ).wait()


def greet_seq(p):
    def body(k, carry):
        greet((p["s"] + k) % SEQ, p["d"])
        return carry

    lax.fori_loop(1, SEQ, body, 0)


ROWS = 144
QX, OX = 8 * 128, 3 * 128
CZ = 256


def x_start(xx):
    q = xx * 27 // 4
    return q - xx // 3, xx * 2


def z_start(ss):
    xx = ss // 8
    q0, o0 = x_start(xx)
    q = ss * 27 // 32
    q = q - ss // 31
    o = ss * 9 // 32
    o = jnp.minimum(o, o0 + 1)
    return q - q0, o - o0


class Reducer:
    def __init__(self, p, which, width, cover, bufs, sems):
        self.p, self.which, self.width, self.cover = p, which, width, cover
        self.lhs_t, self.mine, self.from_core, self.b1 = bufs[:4]
        self.part, self.b2, self.total, self.zbuf = bufs[4:]
        self.pieces = [
            (j, j * cover, min(cover, width - j * cover)) for j in range(-(-width // cover))
        ]
        self.csend, self.crecv, self.s1send, self.s1recv = sems[:4]
        self.s2send, self.s2recv, self.zsend, self.zrecv = sems[4:]
        y, x, s = p["y"], p["x"], p["s"]
        self.order = [(y + k) % 4 for k in (1, 2, 3, 0)]
        self.y_to = [p["zhi"] * 4 + r for r in self.order[:3]]
        self.xs = [(x + k) % 4 for k in (1, 2, 3)]
        self.x_to = [xx * 8 + s % 8 for xx in self.xs]

    def cols(self, xx, t=0, size=None):
        first = x_start(xx)[self.which] * 128
        return pl.ds(pl.multiple_of(first + t, 128), self.cover if size is None else size)

    def core_copy(self, i):
        r = self.order[i]
        p = self.p
        return rcopy(
            self.mine.at[r],
            self.from_core.at[r],
            self.csend.at[i],
            self.crecv.at[i],
            p["s"] + 1 - 2 * p["core"],
            p["d"],
        )

    def first_y(self, i):
        return [
            rcopy(
                self.mine.at[self.order[i], :, pl.ds(at, size)],
                self.b1.at[i * 4 + j, :, pl.ds(0, size)],
                self.s1send.at[i * 4 + j],
                self.s1recv.at[i * 4 + j],
                self.p["s"],
                self.y_to[i],
            )
            for j, at, size in self.pieces
        ]

    def first_x(self, k, i):
        r = self.order[i]
        return rcopy(
            self.mine.at[r, :, self.cols(self.xs[k])],
            self.b1.at[k * 4 + r],
            self.s1send.at[k * 4 + i],
            self.s1recv.at[k * 4 + i],
            self.x_to[k],
            self.p["d"],
        )

    def second_x(self, k):
        return rcopy(
            self.mine.at[self.p["y"], :, self.cols(self.xs[k])],
            self.b2.at[k],
            self.s2send.at[k],
            self.s2recv.at[k],
            self.x_to[k],
            self.p["d"],
        )

    def second_y(self, i):
        return rcopy(
            self.part.at[self.order[i]],
            self.b2.at[i],
            self.s2send.at[i],
            self.s2recv.at[i],
            self.p["s"],
            self.y_to[i],
        )

    def z_target(self, i):
        p = self.p
        ss = p["x"] * 8 + i
        pd = p["core"] * 4 + p["y"]
        at = z_start(ss)[self.which]
        src = self.total.at[:, pl.ds(pl.multiple_of(at * 128, 128), CZ)]
        z_me = p["zhi"] * 4 + p["zlo"]
        return ss, pd, src, z_me

    def z_copy(self, i):
        ss, pd, src, z_me = self.z_target(i)
        return rcopy(src, self.zbuf.at[z_me], self.zsend.at[i], self.zrecv.at[z_me], ss, pd)

    def z_local(self, i):
        ss, pd, src, z_me = self.z_target(i)
        return pltpu.make_async_copy(src, self.zbuf.at[z_me], self.zrecv.at[z_me])

    def product(self, block, rhs_ref, dst, r, add):
        lhs = self.lhs_t[pl.ds(pl.multiple_of(block * ROWS, 16), ROWS), :]
        step = self.width // 9

        def body(t, carry):
            at = pl.ds(pl.multiple_of(t * step, 128), step)
            value = nn(lhs, rhs_ref[:, at]) * GRAD_SCALE
            if add is not None:
                value = value + add[r, :, at].astype(F32)
            dst[r, :, at] = value.astype(BF)
            return carry

        lax.fori_loop(0, 9, body, 0)

    def start(self, load_lhs, rhs_ref):
        def turn(t, carry):
            at = pl.ds(pl.multiple_of(t * 128, 128), 128)
            self.lhs_t[at, :] = load_lhs(at).T
            return carry

        lax.fori_loop(0, 9, turn, 0)
        for i, r in enumerate(self.order):
            self.product((1 - self.p["core"]) * 4 + r, rhs_ref, self.mine, r, None)
            self.core_copy(i).start()

    def first(self, rhs_ref):
        core = self.p["core"]
        for i, r in enumerate(self.order):
            self.core_copy(i).wait()
            self.product(core * 4 + r, rhs_ref, self.mine, r, self.from_core)

            if i < 3:

                @pl.when(core == 0)
                def _():
                    for c in self.first_y(i):
                        c.start()

            @pl.when(core == 1)
            def _():
                for k in range(3):
                    self.first_x(k, i).start()

    def second(self):
        p = self.p
        y = p["y"]

        @pl.when(p["core"] == 0)
        def _():
            for i in range(3):
                for c in self.first_y(i):
                    c.wait_recv()
            n = self.cover // 128

            def body(t, carry):
                at = pl.ds(pl.multiple_of(t * 128, 128), 128)
                there = pl.ds(pl.multiple_of(t % n * 128, 128), 128)
                total = self.mine[y, :, at].astype(F32)
                for i in range(3):
                    total = total + self.b1[i * 4 + t // n, :, there].astype(F32)
                self.mine[y, :, at] = total.astype(BF)
                return carry

            lax.fori_loop(0, self.width // 128, body, 0, unroll=3)
            for k in range(3):
                self.second_x(k).start()

        @pl.when(p["core"] == 1)
        def _():
            for i, r in enumerate(self.order):
                for k in range(3):
                    self.first_x(k, i).wait_recv()

                def body(t, carry):
                    at = pl.ds(pl.multiple_of(t * 128, 128), 128)
                    total = self.mine[r, :, self.cols(p["x"], t * 128, 128)].astype(F32)
                    for k in range(3):
                        total = total + self.b1[k * 4 + r, :, at].astype(F32)
                    self.part[r, :, at] = total.astype(BF)
                    return carry

                lax.fori_loop(0, self.cover // 128, body, 0)
                if i < 3:
                    self.second_y(i).start()

    def third(self):
        p = self.p
        y, x, core = p["y"], p["x"], p["core"]

        def finish(load):
            def body(t, carry):
                at = pl.ds(pl.multiple_of(t * 128, 128), 128)
                total = load(t).astype(F32)
                for k in range(3):
                    total = total + self.b2[k, :, at].astype(F32)
                self.total[:, at] = total.astype(BF)
                return carry

            lax.fori_loop(0, self.cover // 128, body, 0)

        @pl.when(core == 0)
        def _():
            for k in range(3):
                self.second_x(k).wait_recv()
            finish(lambda t: self.mine[y, :, self.cols(x, t * 128, 128)])

        @pl.when(core == 1)
        def _():
            for i in range(3):
                self.second_y(i).wait_recv()
            finish(lambda t: self.part[y, :, pl.ds(pl.multiple_of(t * 128, 128), 128)])

        for i in range(8):
            ss, pd, _, _ = self.z_target(i)
            is_me = jnp.logical_and(ss == p["s"], pd == p["d"])

            @pl.when(jnp.logical_not(is_me))
            def _():
                self.z_copy(i).start()

            @pl.when(is_me)
            def _():
                self.z_local(i).start()

    def last(self, out_ref, size):
        for z in range(8):
            pltpu.make_async_copy(self.zbuf.at[z], self.zbuf.at[z], self.zrecv.at[z]).wait()
        total = self.zbuf[0].astype(F32)
        for z in range(1, 8):
            total = total + self.zbuf[z].astype(F32)
        first = (x_start(self.p["x"])[self.which] + z_start(self.p["s"])[self.which]) * 128
        skip = self.p["s"] * size - first
        out_ref[...] = pltpu.roll(total, (CZ - skip) % CZ, 1)[:, :size]

    def drain(self):
        p = self.p

        @pl.when(p["core"] == 0)
        def _():
            for i in range(3):
                for c in self.first_y(i):
                    c.wait_send()
                self.second_x(i).wait_send()

        @pl.when(p["core"] == 1)
        def _():
            for k in range(3):
                for i in range(4):
                    self.first_x(k, i).wait_send()
                self.second_y(k).wait_send()

        for i in range(8):
            ss, pd, _, _ = self.z_target(i)

            @pl.when(jnp.logical_or(ss != p["s"], pd != p["d"]))
            def _():
                self.z_copy(i).wait_send()


def reducer_scratch(width, cover):
    bufs = [
        pltpu.VMEM((D, 256), BF),
        pltpu.VMEM((4, ROWS, width), BF),
        pltpu.VMEM((4, ROWS, width), BF),
        pltpu.VMEM((12, ROWS, cover), BF),
        pltpu.VMEM((4, ROWS, cover), BF),
        pltpu.VMEM((3, ROWS, cover), BF),
        pltpu.VMEM((ROWS, cover), BF),
        pltpu.VMEM((8, ROWS, CZ), BF),
    ]
    sems = [pltpu.SemaphoreType.DMA((n,)) for n in (4, 4, 12, 12, 3, 3, 8, 8)]
    return bufs + sems


GRAD_SCALE = 1.0 / math.sqrt(DP * SEQ * 256)


SPLIT = 1536
WA, WB = SPLIT // 4, (4 * D - SPLIT) // 4


def whole_kernel(
    w_out_ref,
    w_qkv_ref,
    qkv_ref,
    g_ref,
    spatial_hbm,
    hidden_hbm,
    gout_hbm,
    rows_ref,
    hidden_out,
    spatial_out,
    w_out_out,
    w_qkv_out,
    *scratch,
):
    (
        wall_ref,
        qkvm_ref,
        gm_ref,
        spatial_ref,
        hidden_ref,
        gout_ref,
        attended_ref,
        gqkv_ref,
        wout_ref,
        unit_ref,
        std_ref,
        normed_ref,
        normedm_ref,
        bias_ref,
        gnt_ref,
        gn_ref,
        gnm_ref,
        proj_ref,
        gatt_ref,
        lsem,
        asend,
        arecv,
        wsend,
        wrecv,
    ) = scratch[32:]
    p = position()
    s, d, x, y, core, zhi = p["s"], p["d"], p["x"], p["y"], p["core"], p["zhi"]
    own = [
        pltpu.make_async_copy(w_out_ref, wall_ref.at[d, :, :, pl.ds(0, D)], lsem.at[0]),
        pltpu.make_async_copy(w_qkv_ref, wall_ref.at[d, :, :, pl.ds(D, 3 * D)], lsem.at[4]),
        pltpu.make_async_copy(spatial_hbm, spatial_ref, lsem.at[5]),
        pltpu.make_async_copy(hidden_hbm, hidden_ref, lsem.at[6]),
        pltpu.make_async_copy(gout_hbm, gout_ref, lsem.at[7]),
        pltpu.make_async_copy(qkv_ref.at[s], qkvm_ref.at[s], lsem.at[1]),
        pltpu.make_async_copy(g_ref.at[s], gm_ref.at[s], lsem.at[2]),
    ]
    for c in own:
        c.start()
    greet_seq(p)
    far = (d + 4) % DP
    y_to = [zhi * 4 + (y + k) % 4 for k in (1, 2, 3)]
    y_from = [zhi * 4 + (y + 4 - k) % 4 for k in (1, 2, 3)]
    y_far = [(1 - zhi) * 4 + (y + 4 - k) % 4 for k in (1, 2, 3)]
    x_to = [((x + k) % 4) * 8 + s % 8 for k in (1, 2, 3)]
    x_from = [(x + 4 - k) % 4 for k in (1, 2, 3)]
    sibling = s + 1 - 2 * core
    for peer in y_to:
        greet(s, peer)
    for i in range(8):
        greet(x * 8 + i, (1 - zhi) * 4 + y)
    pl.semaphore_wait(pltpu.get_barrier_semaphore(), SEQ - 1 + 3 + 8)
    own[0].wait()
    own[1].wait()

    rows = pl.ds(core * 9, 9)
    other_rows = pl.ds((1 - core) * 9, 9)

    def col_a(xx):
        return pl.ds(pl.multiple_of(xx * WA, 128), WA)

    def col_b(xx):
        return pl.ds(pl.multiple_of(SPLIT + xx * WB, 128), WB)

    all_b = pl.ds(SPLIT, 4 * WB)
    sent = []
    expected = []

    def send(dd, cols, sem, ps, pd):
        ref = wall_ref.at[dd, rows, :, cols]
        c = rcopy(ref, ref, wsend.at[sem], wrecv.at[sem], ps, pd)
        c.start()
        sent.append(c)

    def arrived(dd, cols, sem, which=None):
        ref = wall_ref.at[dd, rows if which is None else which, :, cols]
        rcopy(ref, ref, wsend.at[sem], wrecv.at[sem], s, far).wait_recv()

    def hand_on(dd, cols, sem):
        send(dd, cols, sem, sibling, d)
        expected.append((dd, cols, sem))

    send(d, col_b(x), 56, s, far)
    send(d, col_a(x), 0, s, far)
    for k in range(3):
        send(d, col_a(x), 1 + k, s, y_to[k])
    for k in range(3):
        send(d, all_b, 60 + k, s, y_to[k])
    pairs = [(qkv_ref, qkvm_ref), (g_ref, gm_ref)]
    a2a_start(p, pairs, asend, arecv)

    arrived(far, col_b(x), 56)
    for k in range(3):
        send(far, col_b(x), 57 + k, x_to[k], d)
    arrived(far, col_a(x), 0)
    for k in range(3):
        send(far, col_a(x), 4 + k, s, y_to[k])
    hand_on(far, col_b(x), 66)

    attended_ref[...] = jnp.zeros_like(attended_ref)
    own[2].wait()

    def spatial(h, carry):
        forward_head(flat_loader(spatial_ref, None), adder(attended_ref), h)
        return carry

    lax.fori_loop(0, HEADS, spatial, 0, unroll=2)

    for k in range(3):
        arrived(far, col_b(x_from[k]), 57 + k)
    for k in range(3):
        send(far, all_b, 63 + k, s, y_to[k])
    for k in range(3):
        hand_on(far, col_b(x_from[k]), 67 + k)
    sources = [far] + y_from + y_far
    for j, dd in enumerate(sources):
        if j:
            arrived(dd, col_a(x), j)
        for k in range(3):
            send(dd, col_a(x), 7 + j * 3 + k, x_to[k], d)
        hand_on(dd, col_a(x), 28 + j)
    for k in range(3):
        arrived(y_from[k], all_b, 60 + k)
        hand_on(y_from[k], all_b, 70 + k)
    for j, dd in enumerate(sources):
        for k in range(3):
            arrived(dd, col_a(x_from[k]), 7 + j * 3 + k)
            hand_on(dd, col_a(x_from[k]), 35 + j * 3 + k)
    for k in range(3):
        arrived(y_far[k], all_b, 63 + k)
        hand_on(y_far[k], all_b, 73 + k)

    at = lax.broadcasted_iota(jnp.int32, (256, 256), 0) % 8
    to = lax.broadcasted_iota(jnp.int32, (256, 256), 1) % 8
    bias_ref[...] = jnp.where(at == to, 0.0, -1e30)
    gqkv_ref[...] = jnp.zeros_like(gqkv_ref)

    own[3].wait()
    for dd, cols, sem in expected:
        if sem < 66:
            arrived(dd, cols, sem, other_rows)

    def assemble(dd, carry):
        at = pl.ds(pl.multiple_of(dd * ROWS, 16), ROWS)
        wout_ref[at, :] = wall_ref[dd, :, :, :D].reshape(ROWS, D)
        return carry

    lax.fori_loop(0, DP, assemble, 0)

    def project(t, carry):
        at = pl.ds(pl.multiple_of(t * 384, 128), 384)
        unit_ref[:, at] = hidden_ref[:, at].astype(F32) + rows_ref[0:1, at] * nn(
            attended_ref[...], wout_ref[:, at]
        )
        return carry

    lax.fori_loop(0, 3, project, 0)

    def normalise(t, carry):
        at = pl.ds(pl.multiple_of(t * 32, 32), 32)
        residual = unit_ref[at, :]
        centered = residual - jnp.mean(residual, axis=-1, keepdims=True)
        inv_std = lax.rsqrt(jnp.mean(centered * centered, axis=-1, keepdims=True) + EPSILON)
        unit = centered * inv_std
        unit_ref[at, :] = unit
        std_ref[at, :] = jnp.broadcast_to(inv_std, (32, 128))
        normed = unit * (1.0 + rows_ref[2:3, :]) + rows_ref[1:2, :]
        normed_ref[pl.ds(t * 4, 4)] = normed.reshape(4, 8, D).astype(BF)
        return carry

    lax.fori_loop(0, 8, normalise, 0)
    own_normed = pltpu.make_async_copy(normed_ref.at[s], normedm_ref.at[s], lsem.at[3])
    own_normed.start()
    normed_pair = [(normed_ref, normedm_ref)]
    a2a_start(p, normed_pair, asend.at[pl.ds(2, 1)], arecv.at[pl.ds(2, 1)])

    a2a_wait(p, pairs, asend, arecv)
    own[5].wait()
    own[6].wait()

    def temporal(h, carry):
        backward_head(block_loader(qkvm_ref, gm_ref), adder(gqkv_ref), h, bias_ref[...])
        return carry

    lax.fori_loop(0, HEADS, temporal, 0, unroll=2)

    for dd, cols, sem in expected:
        if sem >= 66:
            arrived(dd, cols, sem, other_rows)

    def back_project(dd, carry):
        at = pl.ds(pl.multiple_of(dd * ROWS, 16), ROWS)
        gnt_ref[at, :] = nt(wall_ref[dd, :, :, D:].reshape(ROWS, 3 * D), gqkv_ref[...])
        return carry

    lax.fori_loop(0, DP, back_project, 0)

    def turn(t, carry):
        at = pl.ds(pl.multiple_of(t * 128, 128), 128)
        gn_ref[:, :, at] = gnt_ref[at, :].T.reshape(SEQ, 8, 128).astype(BF)
        return carry

    lax.fori_loop(0, 9, turn, 0)
    own_back = pltpu.make_async_copy(gn_ref.at[s], gnm_ref.at[s], lsem.at[8])
    own_back.start()
    back_pair = [(gn_ref, gnm_ref)]
    a2a_start(p, back_pair, asend.at[pl.ds(3, 1)], arecv.at[pl.ds(3, 1)])
    a2a_wait(p, normed_pair, asend.at[pl.ds(2, 1)], arecv.at[pl.ds(2, 1)])
    own_normed.wait()

    rq = Reducer(p, 0, 3 * D, QX, scratch[0:8], scratch[8:16])
    ro = Reducer(p, 1, D, OX, scratch[16:24], scratch[24:32])
    rq.start(lambda at: normedm_ref[:, :, at].reshape(256, 128), gqkv_ref)
    rq.first(gqkv_ref)

    a2a_wait(p, back_pair, asend.at[pl.ds(3, 1)], arecv.at[pl.ds(3, 1)])
    own_back.wait()
    own[4].wait()

    def norm_backward(t, carry):
        at = pl.ds(pl.multiple_of(t * 32, 32), 32)
        unit = unit_ref[at, :]
        inv_std = std_ref[at, 0:1]
        grad_normed = gnm_ref[pl.ds(t * 4, 4)].astype(F32).reshape(32, D)
        grad_hat = grad_normed * (1.0 + rows_ref[2:3, :])
        grad_resid = gout_ref[at, :].astype(F32) + inv_std * (
            grad_hat
            - jnp.mean(grad_hat, axis=-1, keepdims=True)
            - unit * jnp.mean(grad_hat * unit, axis=-1, keepdims=True)
        )
        hidden_out[at, :] = grad_resid.astype(BF)
        proj_ref[at, :] = (rows_ref[0:1, :] * grad_resid).astype(BF)
        return carry

    lax.fori_loop(0, 8, norm_backward, 0)
    ro.start(lambda at: attended_ref[:, at], proj_ref)

    def attend_grad(t, carry):
        at = pl.ds(pl.multiple_of(t * 128, 128), 128)
        gatt_ref[:, at] = nt(proj_ref[...], wout_ref[at, :]).astype(BF)
        return carry

    lax.fori_loop(0, 9, attend_grad, 0)
    ro.first(proj_ref)
    spatial_out[...] = jnp.zeros_like(spatial_out)

    def spatial_back(h, carry):
        backward_head(flat_loader(spatial_ref, gatt_ref), adder(spatial_out), h, None)
        return carry

    lax.fori_loop(0, HEADS // 2, spatial_back, 0, unroll=2)
    rq.second()
    lax.fori_loop(HEADS // 2, HEADS, spatial_back, 0, unroll=2)
    rq.third()
    ro.second()
    ro.third()
    rq.last(w_qkv_out, 108)
    ro.last(w_out_out, 36)
    for c in sent:
        c.wait_send()
    rq.drain()
    ro.drain()


def whole_call(*args):
    any_space = pl.BlockSpec(memory_space=pl.ANY)
    vmem = pl.BlockSpec(memory_space=pltpu.VMEM)
    return pl.pallas_call(
        whole_kernel,
        out_shape=(
            jax.ShapeDtypeStruct((256, D), BF),
            jax.ShapeDtypeStruct((256, 3 * D), BF),
            jax.ShapeDtypeStruct((ROWS, 36), F32),
            jax.ShapeDtypeStruct((ROWS, 108), F32),
        ),
        in_specs=[any_space] * 7 + [vmem],
        out_specs=[vmem] * 4,
        scratch_shapes=reducer_scratch(3 * D, QX)
        + reducer_scratch(D, OX)
        + [
            pltpu.VMEM((DP, 18, 8, 4 * D), BF),
            pltpu.VMEM((SEQ, 8, 3 * D), BF),
            pltpu.VMEM((SEQ, 8, D), BF),
            pltpu.VMEM((256, 3 * D), BF),
            pltpu.VMEM((256, D), BF),
            pltpu.VMEM((256, D), BF),
            pltpu.VMEM((256, D), BF),
            pltpu.VMEM((256, 3 * D), BF),
            pltpu.VMEM((D, D), BF),
            pltpu.VMEM((256, D), F32),
            pltpu.VMEM((256, 128), F32),
            pltpu.VMEM((SEQ, 8, D), BF),
            pltpu.VMEM((SEQ, 8, D), BF),
            pltpu.VMEM((256, 256), F32),
            pltpu.VMEM((D, 256), F32),
            pltpu.VMEM((SEQ, 8, D), BF),
            pltpu.VMEM((SEQ, 8, D), BF),
            pltpu.VMEM((256, D), BF),
            pltpu.VMEM((256, D), BF),
            pltpu.SemaphoreType.DMA((9,)),
            pltpu.SemaphoreType.DMA((4,)),
            pltpu.SemaphoreType.DMA((4,)),
            pltpu.SemaphoreType.DMA((76,)),
            pltpu.SemaphoreType.DMA((76,)),
        ],
        compiler_params=pltpu.CompilerParams(
            collective_id=0, has_side_effects=True, vmem_limit_bytes=VMEM_LIMIT
        ),
        name="whole",
    )(*args)


def per_device(
    hidden_in,
    qkv_spatial,
    qkv_temporal,
    grad_out,
    grad_temporal,
    gate_spatial,
    modulation,
    w_out_spatial,
    w_qkv_temporal,
):
    rows = jnp.concatenate([gate_spatial, modulation[0]], axis=0).astype(F32)
    grad_hidden, grad_qkv_s, grad_w_out, grad_w_qkv = whole_call(
        w_out_spatial.reshape(18, 8, D),
        w_qkv_temporal.reshape(18, 8, 3 * D),
        qkv_temporal.reshape(SEQ, 8, 3 * D),
        grad_temporal.reshape(SEQ, 8, D),
        qkv_spatial.reshape(256, 3 * D),
        hidden_in.reshape(256, D),
        grad_out.reshape(256, D),
        rows,
    )
    return (
        grad_hidden.reshape(hidden_in.shape),
        grad_qkv_s.reshape(qkv_spatial.shape),
        grad_w_out,
        grad_w_qkv,
    )


def solution(mesh):
    in_specs = (
        P("dp", "seq", None, None),
        P("dp", "seq", None, None),
        P("dp", "seq", None, None),
        P("dp", "seq", None, None),
        P("dp", "seq", None, None),
        P("dp", None),
        P("dp", None, None),
        P("dp", None),
        P("dp", None),
    )
    out_specs = (
        P("dp", "seq", None, None),
        P("dp", "seq", None, None),
        P("dp", "seq"),
        P("dp", "seq"),
    )
    return jax.shard_map(
        per_device, mesh=mesh, in_specs=in_specs, out_specs=out_specs, check_vma=False
    )
```

time: 203 us -> 185 us (0.911)
  Pallas kernels: 193 us -> 176 us
    pallas_call x2 -> x1, Pallas kernels: 193 us -> 176 us  [whole_call(): pl.pallas_call(whole_kernel, out_shape=(jax.ShapeDtypeStruct((256, D), BF...]
    unnamed x9 -> x6, local copies, waits for them, and re-layouts: 3.86 us -> 6.98 us
    dynamic_slice x2 -> x0, local copies, waits for them, and re-layouts: 2.75 us -> none  [the longest x1 1.63 us: per_device(): lax.dynamic_slice(sums, (0, 108 * s - 128 * (q_at + q0)), (ROWS, 108))]
    reshape x1 -> x0, other arithmetic: 2.44 us -> none  [per_device(): jnp.concatenate([w_out_spatial, w_qkv_temporal], axis=1)]
where the time goes in v2:
time: 185 us
  Pallas kernels  176 us (95%)
  local copies, waits for them, and re-layouts  6.98 us (4%)
    pallas_call x1, Pallas kernels, whole_call(): pl.pallas_call(whole_kernel, out_shape=(jax.ShapeDtypeStruct((256, D), BF...  176 us
    unnamed x6, local copies, waits for them, and re-layouts  6.98 us

profile of v2, /device:TPU:65, one launch (start us, length us, event | category | flops | bytes accessed | tf_op | source)
XLA Modules:
  0.0 184.6 jit_solution(13973976329790099295)
XLA Ops:
  0.6 1.3 maximum_convert_fusion.rows_ref
  2.0 175.7 %whole.1 = (bf16[256,1152]{1,0:T(8,128)(2,1)}, bf16[256,3456]{1,0:T(8,128)(2,1)}, f32[144,36]{1,0:T(8,128)}, f32[144,108]{1,0:T(8,128)}) custom-call(bf16[18,8,1152]{2,1,0:T(8,128)(2,1)} %bitcast.18, bf16[18,8,3456]{2,1,0:T(8,128)(2,1)} %bitcast.13, bf16[32,8,3456]{2,1,0:T(8,128)(2,1)} %bitcast.10, bf16[32,8,1152]{2,1,0:T(8,128)(2,1)} %bitcast.14, ...), custom_call_target="tpu_custom_call" | custom-call | tf_op jit(solution)/shard_map/whole/pallas_call | solution.py:728
  177.6 1.6 copy.13
  179.2 1.9 %copy.17 = bf16[1,1,256,1152]{3,2,1,0:T(8,128)(2,1)} copy(bf16[1,1,256,1152]{3,2,1,0:T(8,128)(2,1)} %bitcast.17) | data formatting | bytes 1179648
  181.2 0.0 copy-start
  181.2 2.8 %copy.18 = bf16[1,1,256,3456]{3,2,1,0:T(8,128)(2,1)} copy(bf16[1,1,256,3456]{3,2,1,0:T(8,128)(2,1)} %bitcast.12) | data formatting | bytes 3538944
  184.0 0.0 copy-done
  184.0 0.6 copy.19
Async XLA Ops:
  181.2 2.8 %copy-start = (f32[144,108]{1,0:T(8,128)S(1)}, f32[144,108]{1,0:T(8,128)}, u32[]{:S(2)}) copy-start(f32[144,108]{1,0:T(8,128)} %get-tuple-element.23) | copy-start | bytes 186628

commit v3 on v2

--- a/solution.py
+++ b/solution.py
@@ -152,6 +152,7 @@
 ROWS = 144
 QX, OX = 8 * 128, 3 * 128
 CZ = 256
+LANES = 128
 
 
 def x_start(xx):
@@ -172,8 +173,9 @@
 class Reducer:
     def __init__(self, p, which, width, cover, bufs, sems):
         self.p, self.which, self.width, self.cover = p, which, width, cover
+        self.size = width // SEQ
         self.lhs_t, self.mine, self.from_core, self.b1 = bufs[:4]
-        self.part, self.b2, self.total, self.zbuf = bufs[4:]
+        self.part, self.b2, self.total, self.zout, self.zbuf = bufs[4:]
         self.pieces = [
             (j, j * cover, min(cover, width - j * cover)) for j in range(-(-width // cover))
         ]
@@ -249,10 +251,8 @@
         p = self.p
         ss = p["x"] * 8 + i
         pd = p["core"] * 4 + p["y"]
-        at = z_start(ss)[self.which]
-        src = self.total.at[:, pl.ds(pl.multiple_of(at * 128, 128), CZ)]
         z_me = p["zhi"] * 4 + p["zlo"]
-        return ss, pd, src, z_me
+        return ss, pd, self.zout.at[i], z_me
 
     def z_copy(self, i):
         ss, pd, src, z_me = self.z_target(i)
@@ -374,6 +374,15 @@
                 self.second_y(i).wait_recv()
             finish(lambda t: self.part[y, :, pl.ds(pl.multiple_of(t * 128, 128), 128)])
 
+        def pack(i, carry):
+            ss = x * 8 + i
+            at = z_start(ss)[self.which]
+            skip = ss * self.size - (x_start(x)[self.which] + at) * 128
+            value = self.total[:, pl.ds(pl.multiple_of(at * 128, 128), CZ)].astype(F32)
+            self.zout[i] = pltpu.roll(value, (CZ - skip) % CZ, 1)[:, :LANES].astype(BF)
+            return carry
+
+        lax.fori_loop(0, 8, pack, 0)
         for i in range(8):
             ss, pd, _, _ = self.z_target(i)
             is_me = jnp.logical_and(ss == p["s"], pd == p["d"])
@@ -386,15 +395,13 @@
             def _():
                 self.z_local(i).start()
 
-    def last(self, out_ref, size):
+    def last(self, out_ref):
         for z in range(8):
             pltpu.make_async_copy(self.zbuf.at[z], self.zbuf.at[z], self.zrecv.at[z]).wait()
         total = self.zbuf[0].astype(F32)
         for z in range(1, 8):
             total = total + self.zbuf[z].astype(F32)
-        first = (x_start(self.p["x"])[self.which] + z_start(self.p["s"])[self.which]) * 128
-        skip = self.p["s"] * size - first
-        out_ref[...] = pltpu.roll(total, (CZ - skip) % CZ, 1)[:, :size]
+        out_ref[...] = total[:, : self.size]
 
     def drain(self):
         p = self.p
@@ -430,7 +437,8 @@
         pltpu.VMEM((4, ROWS, cover), BF),
         pltpu.VMEM((3, ROWS, cover), BF),
         pltpu.VMEM((ROWS, cover), BF),
-        pltpu.VMEM((8, ROWS, CZ), BF),
+        pltpu.VMEM((8, ROWS, LANES), BF),
+        pltpu.VMEM((8, ROWS, LANES), BF),
     ]
     sems = [pltpu.SemaphoreType.DMA((n,)) for n in (4, 4, 12, 12, 3, 3, 8, 8)]
     return bufs + sems
@@ -483,7 +491,7 @@
         arecv,
         wsend,
         wrecv,
-    ) = scratch[32:]
+    ) = scratch[34:]
     p = position()
     s, d, x, y, core, zhi = p["s"], p["d"], p["x"], p["y"], p["core"], p["zhi"]
     own = [
@@ -668,8 +676,8 @@
     a2a_wait(p, normed_pair, asend.at[pl.ds(2, 1)], arecv.at[pl.ds(2, 1)])
     own_normed.wait()
 
-    rq = Reducer(p, 0, 3 * D, QX, scratch[0:8], scratch[8:16])
-    ro = Reducer(p, 1, D, OX, scratch[16:24], scratch[24:32])
+    rq = Reducer(p, 0, 3 * D, QX, scratch[0:9], scratch[9:17])
+    ro = Reducer(p, 1, D, OX, scratch[17:26], scratch[26:34])
     rq.start(lambda at: normedm_ref[:, :, at].reshape(256, 128), gqkv_ref)
     rq.first(gqkv_ref)
 
@@ -714,8 +722,8 @@
     rq.third()
     ro.second()
     ro.third()
-    rq.last(w_qkv_out, 108)
-    ro.last(w_out_out, 36)
+    rq.last(w_qkv_out)
+    ro.last(w_out_out)
     for c in sent:
         c.wait_send()
     rq.drain()
@@ -728,10 +736,10 @@
     return pl.pallas_call(
         whole_kernel,
         out_shape=(
-            jax.ShapeDtypeStruct((256, D), BF),
-            jax.ShapeDtypeStruct((256, 3 * D), BF),
-            jax.ShapeDtypeStruct((ROWS, 36), F32),
-            jax.ShapeDtypeStruct((ROWS, 108), F32),
+            pltpu.VMEM((256, D), BF),
+            pltpu.VMEM((256, 3 * D), BF),
+            pltpu.VMEM((ROWS, 36), F32),
+            pltpu.VMEM((ROWS, 108), F32),
         ),
         in_specs=[any_space] * 7 + [vmem],
         out_specs=[vmem] * 4,

time: 185 us -> 169 us (0.914)
  Pallas kernels: 176 us -> 164 us
  local copies, waits for them, and re-layouts: 6.98 us -> 3.36 us
    pallas_call x1, Pallas kernels: 176 us -> 164 us  [whole_call(): pl.pallas_call(whole_kernel, out_shape=(pltpu.VMEM((256, D), BF), pltpu.V...]
    unnamed x6 -> x4, local copies, waits for them, and re-layouts: 6.98 us -> 3.36 us
where the time goes in v3:
time: 169 us
  Pallas kernels  164 us (97%)
  local copies, waits for them, and re-layouts  3.36 us (2%)
    pallas_call x1, Pallas kernels, whole_call(): pl.pallas_call(whole_kernel, out_shape=(pltpu.VMEM((256, D), BF), pltpu.V...  164 us

profile of v3, /device:TPU:65, one launch (start us, length us, event | category | flops | bytes accessed | tf_op | source)
XLA Modules:
  0.0 169.1 jit_solution(14097705219761529184)
XLA Ops:
  0.6 1.3 maximum_convert_fusion.rows_ref
  2.0 163.7 %whole.1 = (bf16[256,1152]{1,0:T(8,128)(2,1)S(1)}, bf16[256,3456]{1,0:T(8,128)(2,1)S(1)}, f32[144,36]{1,0:T(8,128)S(1)}, f32[144,108]{1,0:T(8,128)S(1)}) custom-call(bf16[18,8,1152]{2,1,0:T(8,128)(2,1)} %bitcast.18, bf16[18,8,3456]{2,1,0:T(8,128)(2,1)} %bitcast.14, bf16[32,8,3456]{2,1,0:T(8,128)(2,1)} %bitcast.12, bf16[32,8,1152]{2,1,0:T(8,128)(2,1)} %bitcast.15, ...), custom_call_target="tpu_custom_call" | custom-call | tf_op jit(solution)/shard_map/whole/pallas_call | solution.py:736
  165.7 0.8 copy.17
  166.5 1.2 copy.18
  167.7 0.7 copy.13
  168.4 0.6 copy.19

commit v4 on v3

--- a/solution.py
+++ b/solution.py
@@ -262,16 +262,15 @@
         ss, pd, src, z_me = self.z_target(i)
         return pltpu.make_async_copy(src, self.zbuf.at[z_me], self.zrecv.at[z_me])
 
-    def product(self, block, rhs_ref, dst, r, add):
+    def own_product(self, r, rhs_ref):
+        block = self.p["core"] * 4 + r
         lhs = self.lhs_t[pl.ds(pl.multiple_of(block * ROWS, 16), ROWS), :]
         step = self.width // 9
 
         def body(t, carry):
             at = pl.ds(pl.multiple_of(t * step, 128), step)
             value = nn(lhs, rhs_ref[:, at]) * GRAD_SCALE
-            if add is not None:
-                value = value + add[r, :, at].astype(F32)
-            dst[r, :, at] = value.astype(BF)
+            self.mine[r, :, at] = (value + self.from_core[r, :, at].astype(F32)).astype(BF)
             return carry
 
         lax.fori_loop(0, 9, body, 0)
@@ -283,15 +282,24 @@
             return carry
 
         lax.fori_loop(0, 9, turn, 0)
-        for i, r in enumerate(self.order):
-            self.product((1 - self.p["core"]) * 4 + r, rhs_ref, self.mine, r, None)
+        half = pl.ds(pl.multiple_of((1 - self.p["core"]) * 4 * ROWS, 16), 4 * ROWS)
+        step = self.width // 9
+
+        def body(t, carry):
+            at = pl.ds(pl.multiple_of(t * step, 128), step)
+            value = (nn(self.lhs_t[half, :], rhs_ref[:, at]) * GRAD_SCALE).astype(BF)
+            self.mine[:, :, at] = value.reshape(4, ROWS, step)
+            return carry
+
+        lax.fori_loop(0, 9, body, 0)
+        for i in range(4):
             self.core_copy(i).start()
 
     def first(self, rhs_ref):
         core = self.p["core"]
         for i, r in enumerate(self.order):
             self.core_copy(i).wait()
-            self.product(core * 4 + r, rhs_ref, self.mine, r, self.from_core)
+            self.own_product(r, rhs_ref)
 
             if i < 3:
 
@@ -325,7 +333,7 @@
                 self.mine[y, :, at] = total.astype(BF)
                 return carry
 
-            lax.fori_loop(0, self.width // 128, body, 0, unroll=3)
+            lax.fori_loop(0, self.width // 128, body, 0, unroll=9)
             for k in range(3):
                 self.second_x(k).start()
 
@@ -343,7 +351,7 @@
                     self.part[r, :, at] = total.astype(BF)
                     return carry
 
-                lax.fori_loop(0, self.cover // 128, body, 0)
+                lax.fori_loop(0, self.cover // 128, body, 0, unroll=True)
                 if i < 3:
                     self.second_y(i).start()
 
@@ -360,7 +368,7 @@
                 self.total[:, at] = total.astype(BF)
                 return carry
 
-            lax.fori_loop(0, self.cover // 128, body, 0)
+            lax.fori_loop(0, self.cover // 128, body, 0, unroll=True)
 
         @pl.when(core == 0)
         def _():
@@ -382,7 +390,7 @@
             self.zout[i] = pltpu.roll(value, (CZ - skip) % CZ, 1)[:, :LANES].astype(BF)
             return carry
 
-        lax.fori_loop(0, 8, pack, 0)
+        lax.fori_loop(0, 8, pack, 0, unroll=4)
         for i in range(8):
             ss, pd, _, _ = self.z_target(i)
             is_me = jnp.logical_and(ss == p["s"], pd == p["d"])
@@ -459,7 +467,8 @@
     spatial_hbm,
     hidden_hbm,
     gout_hbm,
-    rows_ref,
+    gate_ref,
+    modulation_ref,
     hidden_out,
     spatial_out,
     w_out_out,
@@ -486,6 +495,7 @@
         gnm_ref,
         proj_ref,
         gatt_ref,
+        rows_ref,
         lsem,
         asend,
         arecv,
@@ -565,6 +575,8 @@
         send(far, col_a(x), 4 + k, s, y_to[k])
     hand_on(far, col_b(x), 66)
 
+    rows_ref[0:1, :] = gate_ref[...].astype(F32)
+    rows_ref[1:3, :] = modulation_ref[...].astype(F32)
     attended_ref[...] = jnp.zeros_like(attended_ref)
     own[2].wait()
 
@@ -650,18 +662,19 @@
         backward_head(block_loader(qkvm_ref, gm_ref), adder(gqkv_ref), h, bias_ref[...])
         return carry
 
-    lax.fori_loop(0, HEADS, temporal, 0, unroll=2)
+    lax.fori_loop(0, HEADS, temporal, 0, unroll=4)
 
     for dd, cols, sem in expected:
         if sem >= 66:
             arrived(dd, cols, sem, other_rows)
 
-    def back_project(dd, carry):
-        at = pl.ds(pl.multiple_of(dd * ROWS, 16), ROWS)
-        gnt_ref[at, :] = nt(wall_ref[dd, :, :, D:].reshape(ROWS, 3 * D), gqkv_ref[...])
-        return carry
-
-    lax.fori_loop(0, DP, back_project, 0)
+    def back_project(half, carry):
+        at = pl.ds(pl.multiple_of(half * 4 * ROWS, 16), 4 * ROWS)
+        weights = wall_ref[pl.ds(half * 4, 4), :, :, D:].reshape(4 * ROWS, 3 * D)
+        gnt_ref[at, :] = nt(weights, gqkv_ref[...])
+        return carry
+
+    lax.fori_loop(0, 2, back_project, 0)
 
     def turn(t, carry):
         at = pl.ds(pl.multiple_of(t * 128, 128), 128)
@@ -704,11 +717,11 @@
     ro.start(lambda at: attended_ref[:, at], proj_ref)
 
     def attend_grad(t, carry):
-        at = pl.ds(pl.multiple_of(t * 128, 128), 128)
+        at = pl.ds(pl.multiple_of(t * 384, 128), 384)
         gatt_ref[:, at] = nt(proj_ref[...], wout_ref[at, :]).astype(BF)
         return carry
 
-    lax.fori_loop(0, 9, attend_grad, 0)
+    lax.fori_loop(0, 3, attend_grad, 0)
     ro.first(proj_ref)
     spatial_out[...] = jnp.zeros_like(spatial_out)
 
@@ -741,7 +754,7 @@
             pltpu.VMEM((ROWS, 36), F32),
             pltpu.VMEM((ROWS, 108), F32),
         ),
-        in_specs=[any_space] * 7 + [vmem],
+        in_specs=[any_space] * 7 + [vmem] * 2,
         out_specs=[vmem] * 4,
         scratch_shapes=reducer_scratch(3 * D, QX)
         + reducer_scratch(D, OX)
@@ -765,6 +778,7 @@
             pltpu.VMEM((SEQ, 8, D), BF),
             pltpu.VMEM((256, D), BF),
             pltpu.VMEM((256, D), BF),
+            pltpu.VMEM((3, D), F32),
             pltpu.SemaphoreType.DMA((9,)),
             pltpu.SemaphoreType.DMA((4,)),
             pltpu.SemaphoreType.DMA((4,)),
@@ -789,7 +803,6 @@
     w_out_spatial,
     w_qkv_temporal,
 ):
-    rows = jnp.concatenate([gate_spatial, modulation[0]], axis=0).astype(F32)
     grad_hidden, grad_qkv_s, grad_w_out, grad_w_qkv = whole_call(
         w_out_spatial.reshape(18, 8, D),
         w_qkv_temporal.reshape(18, 8, 3 * D),
@@ -798,7 +811,8 @@
         qkv_spatial.reshape(256, 3 * D),
         hidden_in.reshape(256, D),
         grad_out.reshape(256, D),
-        rows,
+        gate_spatial,
+        modulation.reshape(2, D),
     )
     return (
         grad_hidden.reshape(hidden_in.shape),

time: 169 us -> 162 us (0.959)
  Pallas kernels: 164 us -> 157 us
    pallas_call x1, Pallas kernels: 164 us -> 157 us  [whole_call(): pl.pallas_call(whole_kernel, out_shape=(pltpu.VMEM((256, D), BF), pltpu.V...]
where the time goes in v4:
time: 162 us; the launch traced here: 161 us
  Pallas kernels  157 us (97%)
  local copies, waits for them, and re-layouts  3.36 us (2%)
    pallas_call x1, Pallas kernels, whole_call(): pl.pallas_call(whole_kernel, out_shape=(pltpu.VMEM((256, D), BF), pltpu.V...  157 us
    unnamed x4, local copies, waits for them, and re-layouts  3.36 us

profile of v4, /device:TPU:65, one launch (start us, length us, event | category | flops | bytes accessed | tf_op | source)
XLA Modules:
  0.0 160.9 jit_solution(6003977758339778197)
XLA Ops:
  0.6 156.9 %whole.1 = (bf16[256,1152]{1,0:T(8,128)(2,1)S(1)}, bf16[256,3456]{1,0:T(8,128)(2,1)S(1)}, f32[144,36]{1,0:T(8,128)S(1)}, f32[144,108]{1,0:T(8,128)S(1)}) custom-call(bf16[18,8,1152]{2,1,0:T(8,128)(2,1)} %bitcast.18, bf16[18,8,3456]{2,1,0:T(8,128)(2,1)} %bitcast.14, bf16[32,8,3456]{2,1,0:T(8,128)(2,1)} %bitcast.12, bf16[32,8,1152]{2,1,0:T(8,128)(2,1)} %bitcast.15, ...), custom_call_target="tpu_custom_call" | custom-call | tf_op jit(solution)/shard_map/whole/pallas_call | solution.py:749
  157.6 0.8 copy.17
  158.4 1.2 copy.18
  159.6 0.7 copy.13
  160.3 0.6 copy.19

commit v5 on v4

--- a/solution.py
+++ b/solution.py
@@ -273,7 +273,7 @@
             self.mine[r, :, at] = (value + self.from_core[r, :, at].astype(F32)).astype(BF)
             return carry
 
-        lax.fori_loop(0, 9, body, 0)
+        lax.fori_loop(0, 9, body, 0, unroll=3)
 
     def start(self, load_lhs, rhs_ref):
         def turn(t, carry):
@@ -281,7 +281,7 @@
             self.lhs_t[at, :] = load_lhs(at).T
             return carry
 
-        lax.fori_loop(0, 9, turn, 0)
+        lax.fori_loop(0, 9, turn, 0, unroll=3)
         half = pl.ds(pl.multiple_of((1 - self.p["core"]) * 4 * ROWS, 16), 4 * ROWS)
         step = self.width // 9
 
@@ -291,7 +291,7 @@
             self.mine[:, :, at] = value.reshape(4, ROWS, step)
             return carry
 
-        lax.fori_loop(0, 9, body, 0)
+        lax.fori_loop(0, 9, body, 0, unroll=3)
         for i in range(4):
             self.core_copy(i).start()
 
@@ -599,16 +599,10 @@
         for k in range(3):
             send(dd, col_a(x), 7 + j * 3 + k, x_to[k], d)
         hand_on(dd, col_a(x), 28 + j)
-    for k in range(3):
-        arrived(y_from[k], all_b, 60 + k)
-        hand_on(y_from[k], all_b, 70 + k)
     for j, dd in enumerate(sources):
         for k in range(3):
             arrived(dd, col_a(x_from[k]), 7 + j * 3 + k)
             hand_on(dd, col_a(x_from[k]), 35 + j * 3 + k)
-    for k in range(3):
-        arrived(y_far[k], all_b, 63 + k)
-        hand_on(y_far[k], all_b, 73 + k)
 
     at = lax.broadcasted_iota(jnp.int32, (256, 256), 0) % 8
     to = lax.broadcasted_iota(jnp.int32, (256, 256), 1) % 8
@@ -634,7 +628,7 @@
         )
         return carry
 
-    lax.fori_loop(0, 3, project, 0)
+    lax.fori_loop(0, 3, project, 0, unroll=True)
 
     def normalise(t, carry):
         at = pl.ds(pl.multiple_of(t * 32, 32), 32)
@@ -648,12 +642,18 @@
         normed_ref[pl.ds(t * 4, 4)] = normed.reshape(4, 8, D).astype(BF)
         return carry
 
-    lax.fori_loop(0, 8, normalise, 0)
+    lax.fori_loop(0, 8, normalise, 0, unroll=2)
     own_normed = pltpu.make_async_copy(normed_ref.at[s], normedm_ref.at[s], lsem.at[3])
     own_normed.start()
     normed_pair = [(normed_ref, normedm_ref)]
     a2a_start(p, normed_pair, asend.at[pl.ds(2, 1)], arecv.at[pl.ds(2, 1)])
 
+    for k in range(3):
+        arrived(y_from[k], all_b, 60 + k)
+        hand_on(y_from[k], all_b, 70 + k)
+    for k in range(3):
+        arrived(y_far[k], all_b, 63 + k)
+        hand_on(y_far[k], all_b, 73 + k)
     a2a_wait(p, pairs, asend, arecv)
     own[5].wait()
     own[6].wait()
@@ -681,7 +681,7 @@
         gn_ref[:, :, at] = gnt_ref[at, :].T.reshape(SEQ, 8, 128).astype(BF)
         return carry
 
-    lax.fori_loop(0, 9, turn, 0)
+    lax.fori_loop(0, 9, turn, 0, unroll=3)
     own_back = pltpu.make_async_copy(gn_ref.at[s], gnm_ref.at[s], lsem.at[8])
     own_back.start()
     back_pair = [(gn_ref, gnm_ref)]
@@ -713,7 +713,7 @@
         proj_ref[at, :] = (rows_ref[0:1, :] * grad_resid).astype(BF)
         return carry
 
-    lax.fori_loop(0, 8, norm_backward, 0)
+    lax.fori_loop(0, 8, norm_backward, 0, unroll=2)
     ro.start(lambda at: attended_ref[:, at], proj_ref)
 
     def attend_grad(t, carry):
@@ -721,7 +721,7 @@
         gatt_ref[:, at] = nt(proj_ref[...], wout_ref[at, :]).astype(BF)
         return carry
 
-    lax.fori_loop(0, 3, attend_grad, 0)
+    lax.fori_loop(0, 3, attend_grad, 0, unroll=True)
     ro.first(proj_ref)
     spatial_out[...] = jnp.zeros_like(spatial_out)
 

time: 162 us -> 161 us (level)
  no operation moved by 1% of the time
where the time goes in v5:
time: 161 us; the launch traced here: 160 us
  Pallas kernels  156 us (97%)
  local copies, waits for them, and re-layouts  3.36 us (2%)
    pallas_call x1, Pallas kernels, whole_call(): pl.pallas_call(whole_kernel, out_shape=(pltpu.VMEM((256, D), BF), pltpu.V...  156 us
    unnamed x4, local copies, waits for them, and re-layouts  3.36 us

profile of v5, /device:TPU:65, one launch (start us, length us, event | category | flops | bytes accessed | tf_op | source)
XLA Modules:
  0.0 159.6 jit_solution(6365743132393121412)
XLA Ops:
  0.6 155.6 %whole.1 = (bf16[256,1152]{1,0:T(8,128)(2,1)S(1)}, bf16[256,3456]{1,0:T(8,128)(2,1)S(1)}, f32[144,36]{1,0:T(8,128)S(1)}, f32[144,108]{1,0:T(8,128)S(1)}) custom-call(bf16[18,8,1152]{2,1,0:T(8,128)(2,1)} %bitcast.18, bf16[18,8,3456]{2,1,0:T(8,128)(2,1)} %bitcast.14, bf16[32,8,3456]{2,1,0:T(8,128)(2,1)} %bitcast.12, bf16[32,8,1152]{2,1,0:T(8,128)(2,1)} %bitcast.15, ...), custom_call_target="tpu_custom_call" | custom-call | tf_op jit(solution)/shard_map/whole/pallas_call | solution.py:749
  156.2 0.8 copy.17
  157.1 1.2 copy.18
  158.3 0.7 copy.13
  159.0 0.6 copy.19

commit v6 on v5

--- a/solution.py
+++ b/solution.py
@@ -558,21 +558,21 @@
         send(dd, cols, sem, sibling, d)
         expected.append((dd, cols, sem))
 
-    send(d, col_b(x), 56, s, far)
     send(d, col_a(x), 0, s, far)
     for k in range(3):
         send(d, col_a(x), 1 + k, s, y_to[k])
+    send(d, col_b(x), 56, s, far)
     for k in range(3):
         send(d, all_b, 60 + k, s, y_to[k])
     pairs = [(qkv_ref, qkvm_ref), (g_ref, gm_ref)]
     a2a_start(p, pairs, asend, arecv)
 
+    arrived(far, col_a(x), 0)
+    for k in range(3):
+        send(far, col_a(x), 4 + k, s, y_to[k])
     arrived(far, col_b(x), 56)
     for k in range(3):
         send(far, col_b(x), 57 + k, x_to[k], d)
-    arrived(far, col_a(x), 0)
-    for k in range(3):
-        send(far, col_a(x), 4 + k, s, y_to[k])
     hand_on(far, col_b(x), 66)
 
     rows_ref[0:1, :] = gate_ref[...].astype(F32)
@@ -586,12 +586,6 @@
 
     lax.fori_loop(0, HEADS, spatial, 0, unroll=2)
 
-    for k in range(3):
-        arrived(far, col_b(x_from[k]), 57 + k)
-    for k in range(3):
-        send(far, all_b, 63 + k, s, y_to[k])
-    for k in range(3):
-        hand_on(far, col_b(x_from[k]), 67 + k)
     sources = [far] + y_from + y_far
     for j, dd in enumerate(sources):
         if j:
@@ -599,6 +593,12 @@
         for k in range(3):
             send(dd, col_a(x), 7 + j * 3 + k, x_to[k], d)
         hand_on(dd, col_a(x), 28 + j)
+    for k in range(3):
+        arrived(far, col_b(x_from[k]), 57 + k)
+    for k in range(3):
+        send(far, all_b, 63 + k, s, y_to[k])
+    for k in range(3):
+        hand_on(far, col_b(x_from[k]), 67 + k)
     for j, dd in enumerate(sources):
         for k in range(3):
             arrived(dd, col_a(x_from[k]), 7 + j * 3 + k)

time: 161 us -> 160 us (level)
  no operation moved by 1% of the time
where the time goes in v6:
time: 160 us; the launch traced here: 159 us
  Pallas kernels  155 us (97%)
  local copies, waits for them, and re-layouts  3.36 us (2%)
    pallas_call x1, Pallas kernels, whole_call(): pl.pallas_call(whole_kernel, out_shape=(pltpu.VMEM((256, D), BF), pltpu.V...  155 us
    unnamed x4, local copies, waits for them, and re-layouts  3.36 us

profile of v6, /device:TPU:65, one launch (start us, length us, event | category | flops | bytes accessed | tf_op | source)
XLA Modules:
  0.0 159.1 jit_solution(12903498148870722464)
XLA Ops:
  0.6 155.0 %whole.1 = (bf16[256,1152]{1,0:T(8,128)(2,1)S(1)}, bf16[256,3456]{1,0:T(8,128)(2,1)S(1)}, f32[144,36]{1,0:T(8,128)S(1)}, f32[144,108]{1,0:T(8,128)S(1)}) custom-call(bf16[18,8,1152]{2,1,0:T(8,128)(2,1)} %bitcast.18, bf16[18,8,3456]{2,1,0:T(8,128)(2,1)} %bitcast.14, bf16[32,8,3456]{2,1,0:T(8,128)(2,1)} %bitcast.12, bf16[32,8,1152]{2,1,0:T(8,128)(2,1)} %bitcast.15, ...), custom_call_target="tpu_custom_call" | custom-call | tf_op jit(solution)/shard_map/whole/pallas_call | solution.py:749
  155.7 0.8 copy.17
  156.5 1.2 copy.18
  157.7 0.7 copy.13
  158.4 0.6 copy.19
